TPU v7x, 32 devices: a whole 2x2x4 slice. The times are simulated.
32 devices in a mesh: row: 8 (over z, y), col: 4 (over x, core).
Axes of the slice: x: 2, y: 2, z: 4, core: 2. Of those that a mesh axis runs over, the one named last changes fastest.
Arguments:
- edit_keys: bfloat16 [256, 14336], P('row', 'col'), may hold values from -6.75 to 6.75
- edit_shifts: bfloat16 [256, 4096], P('row', 'col'), may hold values from -6 to 6
- ridge_scale: float32 [1], replicated, may hold values from 0.5 to 2
Outputs:
- panel_a: float32 [14336, 256], P('row')
- panel_b: float32 [14336, 256], P('row')
- trailing: float32 [14336, 14336], P('row', 'col')
- forward: float32 [14336, 4096], P('row', 'col')
All inputs are finite; a program needn't handle non-finite values.
Results may differ from a plain program's by a relative error of at most 0.0003.
Values may be sent and summed in bfloat16 or wider, within the bound.
No kernel may reach another device: no remote copies, remote signals or barrier semaphores. Data moves between devices by JAX's collectives and lax.ppermute only.
A program may use at most 128 MiB of HBM per device.

v0:
```python
import functools
import jax
import jax.numpy as jnp
from jax import lax
from jax.experimental import pallas as pl
from jax.experimental.pallas import tpu as pltpu
from jax.sharding import PartitionSpec as P

PANEL = 256
CHUNK = 128
GROUP = 64
WIDTH = 256
SLOTS = 3
EXACT = lax.Precision.HIGHEST
VMEM = pl.BlockSpec(memory_space=pltpu.VMEM)
SMEM = pl.BlockSpec(memory_space=pltpu.SMEM)
ANY = pl.BlockSpec(memory_space=pl.ANY)


def iota(shape, dim):
    return lax.broadcasted_iota(jnp.int32, shape, dim)


def product(left_side, right_side, left_dim, right_dim, precision=None):
    return lax.dot_general(
        left_side,
        right_side,
        (((left_dim,), (right_dim,)), ((), ())),
        precision=precision,
        preferred_element_type=jnp.float32,
    )


def split_three(value):
    high = value.astype(jnp.bfloat16)
    rest = value - high.astype(jnp.float32)
    middle = rest.astype(jnp.bfloat16)
    low = (rest - middle.astype(jnp.float32)).astype(jnp.bfloat16)
    return high, middle, low


def store_sums(out_ref, top, sums):
    high, middle, low = (term.astype(jnp.float32) for term in split_three(sums))
    upper = jnp.concatenate([high, middle], axis=1)
    lower = jnp.concatenate([low, jnp.zeros_like(low)], axis=1)
    out_ref[top : top + 16, 0:256] = jnp.concatenate([upper, lower], axis=0).astype(jnp.bfloat16)


def load_sums(rows):
    wide = rows.astype(jnp.float32)
    return wide[0:8, 0:128] + wide[0:8, 128:256] + wide[8:16, 0:128]


def pack_kernel(keys_ref, out_ref):
    rows, units = keys_ref.shape
    out_ref[0:rows, :] = keys_ref[:, 0:PANEL]
    sums = jnp.zeros((8, 128), jnp.float32)
    for lane in range(0, units, 128):
        wide = keys_ref[:, lane : lane + 128].astype(jnp.float32)
        squares = wide * wide
        for top in range(0, rows, 8):
            sums = sums + squares[top : top + 8]
    store_sums(out_ref, rows, sums)


def merge_kernel(gathered_ref, out_ref):
    cols, rows, _ = gathered_ref.shape
    rows = rows - 16
    out_ref[...] = jnp.zeros(out_ref.shape, out_ref.dtype)
    out_ref[0:rows, 0:PANEL] = gathered_ref[0, 0:rows, :]
    out_ref[0:rows, PANEL : 2 * PANEL] = gathered_ref[1, 0:rows, :]
    sums = jnp.zeros((8, 128), jnp.float32)
    for col in range(cols):
        sums = sums + load_sums(gathered_ref[col, rows : rows + 16, :])
    store_sums(out_ref, rows, sums)


def factor_group(tiles, base):
    lane = iota((8, 128), 1)
    sub = iota((8, 128), 0)
    diagonals = []
    for top in range(len(tiles)):
        live = range(top, len(tiles))
        first = base + 8 * top
        columns = [
            {at: jnp.broadcast_to(tiles[at][:, first + q : first + q + 1], (8, 128)) for at in live}
            for q in range(8)
        ]
        scale = jnp.zeros((8, 128), jnp.float32)
        pivots = jnp.zeros((8, 128), jnp.float32)
        for q in range(8):
            column = columns[q]
            pivot = jnp.broadcast_to(column[top][q : q + 1, :], (8, 128))
            inverse = 1.0 / pivot
            for k in range(q + 1, 8):
                factor = jnp.broadcast_to(column[top][k : k + 1, :], (8, 128)) * inverse
                for at in live:
                    columns[k][at] = columns[k][at] - column[at] * factor
            row = jnp.broadcast_to(tiles[top][q : q + 1, :], (8, 128))
            row = jnp.where(lane == first + q, 1.0, row)
            scaled = row * inverse
            for at in live:
                kept = jnp.where(lane == first + q, 0.0, tiles[at])
                new = kept - column[at] * scaled
                if at == top:
                    new = jnp.where(sub < q, tiles[at], jnp.where(sub == q, row, new))
                tiles[at] = new
            scale = jnp.where(sub == q, lax.rsqrt(pivot), scale)
            pivots = jnp.where(sub == q, pivot, pivots)
        tiles[top] = tiles[top] * scale
        diagonals.append(pivots * scale)
    return tiles, diagonals


def factor_chunk(work):
    lane = iota((CHUNK, CHUNK), 1)
    row = iota((CHUNK, CHUNK), 0)
    diagonals = []
    for base in range(0, CHUNK, GROUP):
        rest = base + GROUP
        tiles = [work[top : top + 8, :] for top in range(base, rest, 8)]
        tiles, found = factor_group(tiles, base)
        diagonals += found
        done = jnp.concatenate(tiles, axis=0)
        work[base:rest, :] = done
        if rest < CHUNK:
            group_lane = lane[base:rest]
            upper = (group_lane > row[base:rest]) & (group_lane < rest)
            update = product(done, jnp.where(upper, 0.0, done), 0, 0, EXACT)[rest:]
            later_lane = lane[rest:]
            own = (later_lane >= base) & (later_lane < rest)
            work[rest:, :] = jnp.where(own, 0.0, work[rest:, :]) - update
    both = work[...]
    diagonal = jnp.concatenate(diagonals, axis=0)
    inverse = jnp.where(lane <= row, both, 0.0)
    factor = jnp.where(lane > row, both, jnp.where(lane == row, diagonal, 0.0))
    return inverse, factor


def eliminate_kernel(
    total_units, ids_ref, ridge_ref, packed_ref, amount_ref, lower_ref, vectors_ref, middle_ref, keys, work
):
    shards = packed_ref.shape[0]
    rows = packed_ref.shape[1] - 16
    own = ids_ref[0]
    sums = jnp.zeros((8, 128), jnp.float32)
    for shard in range(shards):
        keys[shard * rows : (shard + 1) * rows, :] = packed_ref[own ^ shard, 0:rows, :]
        sums = sums + load_sums(packed_ref[shard, rows : rows + 16, 0:256])
    total = jnp.sum(jnp.sum(sums, axis=0, keepdims=True), axis=1, keepdims=True)
    amount = total * ridge_ref[0] / total_units
    amount_ref[...] = jnp.broadcast_to(amount, amount_ref.shape)
    held = keys[...]
    depth = held.shape[0]
    chunks = 2 * PANEL // CHUNK
    gram = product(held, held, 0, 0)
    flipped = held.astype(jnp.float32).T
    square = (CHUNK, CHUNK)
    ridge = jnp.where(iota(square, 0) == iota(square, 1), jnp.broadcast_to(amount, square), 0.0)
    solved = []
    factors = []
    middle = jnp.where(iota((depth, depth), 0) == iota((depth, depth), 1), 1.0, 0.0)
    for chunk in range(chunks):
        low, high = chunk * CHUNK, (chunk + 1) * CHUNK
        block = gram[low:high, low:high] + ridge
        for row in solved:
            block = block - product(row[:, low:high], row[:, low:high], 0, 0, EXACT)
        work[chunk] = block
        later = flipped[low:high, :]
        if high < gram.shape[1]:
            later = jnp.concatenate([gram[low:high, high:], later], axis=1)
        for row in solved:
            later = later - product(row[:, low:high], row[:, high:], 0, 0, EXACT)
        inverse, factor = factor_chunk(work.at[chunk])
        later = product(inverse, later, 1, 0, EXACT)
        solved.append(jnp.concatenate([jnp.zeros((CHUNK, high), jnp.float32), later], axis=1))
        factors.append(factor)
        vector = later[:, -depth:]
        vectors_ref[:, low:high] = vector.T
        middle = middle - product(vector, vector, 0, 0, EXACT)
    middle_ref[...] = middle
    for panel in range(2):
        first = 2 * panel
        left = first * CHUNK
        side = solved[first][:, left + CHUNK : left + 2 * CHUNK]
        upper = jnp.concatenate([factors[first], side], axis=1)
        under = jnp.concatenate([jnp.zeros(square, jnp.float32), factors[first + 1]], axis=1)
        lower_ref[panel] = jnp.concatenate([upper, under], axis=0).T


def tile_kernel(
    sizes,
    ids_ref,
    amount_ref,
    lower_ref,
    vectors_ref,
    middle_ref,
    row_keys_ref,
    right_ref,
    panel_a_ref,
    panel_b_ref,
    trailing_ref,
    forward_ref,
    left,
    right,
    terms,
    out,
    sems,
):
    band, col_units, steps = sizes
    step = pl.program_id(0)
    slot = lax.rem(step, SLOTS)
    row_index = ids_ref[0]
    col_index = ids_ref[1]
    depth, row_units = row_keys_ref.shape
    col_steps = col_units // WIDTH
    block = step - 2

    @pl.when(step == 0)
    def _():
        flipped = row_keys_ref[...].astype(jnp.float32).T.astype(jnp.bfloat16)
        left[:, 0:depth] = flipped
        left[:, depth : 2 * depth] = flipped
        for place, term in enumerate(split_three(middle_ref[...])):
            terms[place] = term

    def put_right(value):
        high = value.astype(jnp.bfloat16)
        right[0:depth, :] = high
        right[depth : 2 * depth, :] = (value - high.astype(jnp.float32)).astype(jnp.bfloat16)

    @pl.when(step < 2)
    def _():
        put_right(vectors_ref[:, pl.ds(pl.multiple_of(step * PANEL, PANEL), PANEL)])

    @pl.when(step >= 2)
    def _():
        keys = right_ref[...]
        value = product(terms[2], keys, 1, 0) + product(terms[1], keys, 1, 0)
        put_right(value + product(terms[0], keys, 1, 0))

    def copy_out(target):
        return pltpu.make_async_copy(out.at[slot], target, sems.at[slot])

    @pl.when(step >= SLOTS)
    def _():
        copy_out(panel_a_ref).wait()

    out[slot] = product(left[...], right[...], 1, 0)

    in_a = row_index == 0
    in_b = row_index == band
    zeros = jnp.zeros((PANEL, WIDTH), jnp.float32)

    @pl.when((step == 0) & in_a)
    def _():
        out[slot, 0:PANEL, :] = lower_ref[0]

    @pl.when((step == 1) & in_a)
    def _():
        out[slot, 0:PANEL, :] = zeros

    @pl.when((step == 1) & in_b)
    def _():
        out[slot, 0:PANEL, :] = lower_ref[1]

    is_trailing = (block >= 0) & (block < col_steps)
    is_forward = block >= col_steps
    apart = col_index * col_units + block * WIDTH - row_index * row_units

    @pl.when(is_trailing & (apart > -WIDTH) & (apart < row_units))
    def _():
        top = pl.multiple_of(jnp.clip(apart, 0, row_units - WIDTH), 64)
        square = (WIDTH, WIDTH)
        near = iota(square, 0) + (top - apart) == iota(square, 1)
        amount = jnp.broadcast_to(amount_ref[0:1, 0:1], square)
        held = out[slot, pl.ds(top, WIDTH), :]
        out[slot, pl.ds(top, WIDTH), :] = held + jnp.where(near, amount, 0.0)

    @pl.when(is_trailing & (in_a | in_b))
    def _():
        out[slot, 0:PANEL, :] = zeros

    @pl.when((block == 0) & (col_index < 2))
    def _():
        out[slot] = jnp.zeros((row_units, WIDTH), jnp.float32)

    @pl.when(is_forward & (in_a | in_b))
    def _():
        first = pl.multiple_of(jnp.where(in_a, 0, PANEL), PANEL)
        vectors = vectors_ref[:, pl.ds(first, PANEL)].T
        high, mid, low = split_three(vectors)
        shifts = right_ref[...]
        value = product(low, shifts, 1, 0) + product(mid, shifts, 1, 0)
        out[slot, 0:PANEL, :] = value + product(high, shifts, 1, 0)

    @pl.when(step == 0)
    def _():
        copy_out(panel_a_ref).start()

    @pl.when(step == 1)
    def _():
        copy_out(panel_b_ref).start()

    @pl.when(is_trailing)
    def _():
        at = pl.multiple_of(block * WIDTH, WIDTH)
        copy_out(trailing_ref.at[:, pl.ds(at, WIDTH)]).start()

    @pl.when(is_forward)
    def _():
        at = pl.multiple_of((block - col_steps) * WIDTH, WIDTH)
        copy_out(forward_ref.at[:, pl.ds(at, WIDTH)]).start()

    @pl.when(step == steps - 1)
    def _():
        for place in range(SLOTS):
            pltpu.make_async_copy(out.at[place], panel_a_ref, sems.at[place]).wait()


def double_up(block, axis, count):
    step = 1
    while step < count:
        pairs = [(place, place ^ step) for place in range(count)]
        block = jnp.concatenate([block, lax.ppermute(block, axis, pairs)], axis=0)
        step *= 2
    return block


def on_device(edit_keys, edit_shifts, ridge_scale):
    row_count = lax.axis_size("row")
    col_count = lax.axis_size("col")
    row_index = lax.axis_index("row")
    col_index = lax.axis_index("col")
    rows, col_units = edit_keys.shape
    shift_cols = edit_shifts.shape[1]
    depth = rows * row_count
    total_units = col_units * col_count
    row_units = total_units // row_count
    band = row_count // col_count
    ids = jnp.stack([row_index, col_index]).astype(jnp.int32)

    rights = lax.all_gather(
        jnp.concatenate([edit_keys, edit_shifts], axis=1), "row", axis=0, tiled=True
    )

    pieces = []
    for turn in range(band):
        part = (row_index + turn) % band
        piece = lax.dynamic_slice_in_dim(edit_keys, part * row_units, row_units, 1)
        pairs = []
        for row in range(row_count):
            for col in range(col_count):
                target = (col * band + (row + turn) % band) * col_count + row // band
                pairs.append((row * col_count + col, target))
        pieces.append(lax.ppermute(piece, ("row", "col"), pairs))

    packed = pl.pallas_call(
        pack_kernel,
        out_shape=jax.ShapeDtypeStruct((rows + 16, PANEL), jnp.bfloat16),
        in_specs=[VMEM],
        out_specs=VMEM,
    )(edit_keys)
    merged = pl.pallas_call(
        merge_kernel,
        out_shape=jax.ShapeDtypeStruct((rows + 16, 2 * PANEL), jnp.bfloat16),
        in_specs=[VMEM],
        out_specs=VMEM,
    )(lax.all_gather(packed, "col", axis=0))
    everyone = double_up(merged[None], "row", row_count)

    amount, lower, vectors, middle = pl.pallas_call(
        functools.partial(eliminate_kernel, total_units),
        out_shape=(
            jax.ShapeDtypeStruct((8, 128), jnp.float32),
            jax.ShapeDtypeStruct((2, PANEL, PANEL), jnp.float32),
            jax.ShapeDtypeStruct((depth, 2 * PANEL), jnp.float32),
            jax.ShapeDtypeStruct((depth, depth), jnp.float32),
        ),
        in_specs=[SMEM, SMEM, VMEM],
        out_specs=(VMEM, VMEM, VMEM, VMEM),
        scratch_shapes=[
            pltpu.VMEM((depth, 2 * PANEL), jnp.bfloat16),
            pltpu.VMEM((2 * PANEL // CHUNK, CHUNK, CHUNK), jnp.float32),
        ],
        compiler_params=pltpu.CompilerParams(vmem_limit_bytes=32 * 2**20),
        cost_estimate=pl.CostEstimate(flops=2 * 10**10, bytes_accessed=10**6, transcendentals=0),
    )(ids, ridge_scale, everyone)

    part = row_index % band
    stacked = jnp.stack(pieces)
    ordered = [
        lax.dynamic_index_in_dim(stacked, (part - place) % band, 0, keepdims=False)
        for place in range(band)
    ]
    row_keys = lax.all_gather(jnp.concatenate(ordered, axis=0), "col", axis=0, tiled=True)

    col_steps = col_units // WIDTH
    steps = 2 + col_steps + shift_cols // WIDTH
    return tuple(
        pl.pallas_call(
            functools.partial(tile_kernel, (band, col_units, steps)),
            grid=(steps,),
            out_shape=(
                jax.ShapeDtypeStruct((row_units, PANEL), jnp.float32),
                jax.ShapeDtypeStruct((row_units, PANEL), jnp.float32),
                jax.ShapeDtypeStruct((row_units, col_units), jnp.float32),
                jax.ShapeDtypeStruct((row_units, shift_cols), jnp.float32),
            ),
            in_specs=[
                SMEM,
                VMEM,
                VMEM,
                VMEM,
                VMEM,
                VMEM,
                pl.BlockSpec((depth, WIDTH), lambda step: (0, jnp.maximum(step - 2, 0))),
            ],
            out_specs=(ANY, ANY, ANY, ANY),
            scratch_shapes=[
                pltpu.VMEM((row_units, 2 * depth), jnp.bfloat16),
                pltpu.VMEM((2 * depth, WIDTH), jnp.bfloat16),
                pltpu.VMEM((3, depth, depth), jnp.bfloat16),
                pltpu.VMEM((SLOTS, row_units, WIDTH), jnp.float32),
                pltpu.SemaphoreType.DMA((SLOTS,)),
            ],
            compiler_params=pltpu.CompilerParams(vmem_limit_bytes=40 * 2**20),
            cost_estimate=pl.CostEstimate(
                flops=10**10, bytes_accessed=4 * 10**7, transcendentals=0
            ),
        )(ids, amount, lower, vectors, middle, row_keys, rights)
    )


def solution(mesh):
    return jax.shard_map(
        on_device,
        mesh=mesh,
        in_specs=(P("row", "col"), P("row", "col"), P()),
        out_specs=(P("row", None), P("row", None), P("row", "col"), P("row", "col")),
        check_vma=False,
    )
```

profile of v0, /device:TPU:0, one launch (start us, length us, event | category | flops | bytes accessed | tf_op | source)
XLA Modules:
  0.0 112.3 jit_solution(12435431927512116818)
XLA Ops:
  7.2 0.0 all-gather.3.cloned.1.call-start
  7.2 1.7 %pad_maximum_fusion.1 = bf16[32,4608]{1,0:T(8,128)(2,1)} fusion(bf16[32,1024]{1,0:T(8,128)(2,1)} %param.4, bf16[32,3584]{1,0:T(8,128)(2,1)} %keys_ref.1), kind=kLoop, calls=%fused_computation.1 | loop fusion | flops 589824 | bytes 589824 | tf_op jit(solution)/shard_map/concatenate | solution.py:344
  8.9 0.0 all-gather.3.cloned.1.call-update
  8.9 1.7 %shard_map.66 = bf16[48,256]{1,0:T(8,128)(2,1)} custom-call(bf16[32,3584]{1,0:T(8,128)(2,1)} %keys_ref.1), custom_call_target="tpu_custom_call" | custom-call | tf_op jit(solution)/shard_map/pallas_call | solution.py:358
  10.6 8.2 %all-gather = bf16[192,256]{1,0:T(8,128)(2,1)} all-gather(bf16[48,256]{1,0:T(8,128)(2,1)} %shard_map.66), channel_id=2, replica_groups=mesh['row'=8,'col'=4] {'col'}, dimensions={0}, use_global_device_ids=true | all-gather | bytes 122880 | tf_op jit(solution)/shard_map/all_gather | solution.py:369
  18.8 1.5 %shard_map.67 = bf16[48,512]{1,0:T(8,128)(2,1)} custom-call(bf16[4,48,256]{2,1,0:T(8,128)(2,1)} %bitcast.14), custom_call_target="tpu_custom_call" | custom-call | tf_op jit(solution)/shard_map/pallas_call | solution.py:364
  20.4 0.0 copy-start.1
  20.4 1.5 %collective-permute-start = (bf16[1,48,512]{2,1,0:T(8,128)(2,1)}, bf16[1,48,512]{2,1,0:T(8,128)(2,1)S(1)}, u32[]{:S(2)}, u32[]{:S(2)}) collective-permute-start(bf16[1,48,512]{2,1,0:T(8,128)(2,1)} %bitcast.10), channel_id=1, source_target_pairs={{0,4},{4,0},{8,12},{12,8},{16,20},{20,16},{24,28},{28,24},{1,5},{5... | collective-permute-start | bytes 147464 | tf_op jit(solution)/shard_map/ppermute | solution.py:325
  21.9 1.0 constant_dynamic-slice_fusion
  22.9 0.6 collective-permute-start.4
  23.4 0.7 collective-permute-start.3
  24.1 0.1 pad_add_fusion.ids_ref
  24.8 0.8 collective-permute-done
  25.6 0.8 pad_maximum_fusion.4
  26.4 3.3 %collective-permute-start.1 = (bf16[2,48,512]{2,1,0:T(8,128)(2,1)S(1)}, bf16[2,48,512]{2,1,0:T(8,128)(2,1)S(1)}, u32[]{:S(2)}, u32[]{:S(2)}) collective-permute-start(bf16[2,48,512]{2,1,0:T(8,128)(2,1)S(1)} %pad_maximum_fusion.4), channel_id=1, source_target_pairs={{0,8},{4,12},{8,0},{12,4},{16,24},{20,28},{24,16},{28,20},{1,9},{5... | collective-permute-start | bytes 294920 | tf_op jit(solution)/shard_map/ppermute | solution.py:325
  29.7 0.4 collective-permute-done.4
  30.2 0.0 collective-permute-done.3
  30.2 0.1 fusion.3
  30.3 11.0 %collective-permute-done.1 = bf16[2,48,512]{2,1,0:T(8,128)(2,1)S(1)} collective-permute-done((bf16[2,48,512]{2,1,0:T(8,128)(2,1)S(1)}, bf16[2,48,512]{2,1,0:T(8,128)(2,1)S(1)}, u32[]{:S(2)}, u32[]{:S(2)}) %collective-permute-start.1) | collective-permute-done | bytes 98336 | tf_op jit(solution)/shard_map/ppermute | solution.py:325
  41.3 0.8 pad_maximum_fusion.3
  42.1 3.1 %collective-permute-start.2 = (bf16[4,48,512]{2,1,0:T(8,128)(2,1)S(1)}, bf16[4,48,512]{2,1,0:T(8,128)(2,1)S(1)}, u32[]{:S(2)}, u32[]{:S(2)}) collective-permute-start(bf16[4,48,512]{2,1,0:T(8,128)(2,1)S(1)} %pad_maximum_fusion.3), channel_id=1, source_target_pairs={{0,16},{4,20},{8,24},{12,28},{16,0},{20,4},{24,8},{28,12},{1,17},{... | collective-permute-start | bytes 589832 | tf_op jit(solution)/shard_map/ppermute | solution.py:325
  45.2 10.1 %all_gather.14.row_keys_ref = bf16[256,1792]{1,0:T(8,128)(2,1)S(1)} all-gather(bf16[64,1792]{1,0:T(8,128)(2,1)S(1)} %pad_maximum_fusion.2), channel_id=1, replica_groups=mesh['row'=8,'col'=4] {'col'}, dimensions={0}, use_global_device_ids=true | all-gather | bytes 1146880 | tf_op jit(solution)/shard_map/all_gather | solution.py:396
  55.3 6.0 %collective-permute-done.2 = bf16[4,48,512]{2,1,0:T(8,128)(2,1)S(1)} collective-permute-done((bf16[4,48,512]{2,1,0:T(8,128)(2,1)S(1)}, bf16[4,48,512]{2,1,0:T(8,128)(2,1)S(1)}, u32[]{:S(2)}, u32[]{:S(2)}) %collective-permute-start.2) | collective-permute-done | bytes 196640 | tf_op jit(solution)/shard_map/ppermute | solution.py:325
  61.3 0.0 copy-done.1
  61.3 18.7 %shard_map.68 = (f32[8,128]{1,0:T(8,128)S(1)}, f32[2,256,256]{2,1,0:T(8,128)S(1)}, f32[256,512]{1,0:T(8,128)S(1)}, f32[256,256]{1,0:T(8,128)S(1)}) custom-call(s32[2]{0:T(128)S(1)} %pad_add_fusion.ids_ref, f32[1]{0:T(128)S(6)} %copy.7.ridge_ref, bf16[8,48,512]{2,1,0:T(8,128)(2,1)S(1)} %pad_maximum_fusion.packed_ref), custom_call_target="tpu_custom_call" | custom-call | flops 20000000000 | bytes 1000000 | tf_op jit(solution)/shard_map/pallas_call | solution.py:372
  80.1 0.0 all-gather.3.cloned.1.call-done.right_ref
  80.1 0.0 copy-start
  80.1 1.7 %copy-done = bf16[256,4608]{1,0:T(8,128)(2,1)S(1)} copy-done((bf16[256,4608]{1,0:T(8,128)(2,1)S(1)}, bf16[256,4608]{1,0:T(8,128)(2,1)}, u32[]{:S(2)}) %copy-start) | copy-done | bytes 2359320
  81.8 23.7 %shard_map.69 = (f32[1792,256]{1,0:T(8,128)}, f32[1792,256]{1,0:T(8,128)}, f32[1792,3584]{1,0:T(8,128)}, f32[1792,1024]{1,0:T(8,128)}) custom-call(s32[2]{0:T(128)S(1)} %pad_add_fusion.ids_ref, f32[8,128]{1,0:T(8,128)S(1)} %get-tuple-element.8.amount_ref, f32[2,256,256]{2,1,0:T(8,128)S(1)} %get-tuple-element.9.lower_ref, ...), custom_call_target="tpu_custom_call" | custom-call | flops 10000000000 | bytes 40000000 | tf_op jit(solution)/shard_map/pallas_call | solution.py:401
  (2 shorter events, 0.1 us)
Async XLA Ops:
  7.2 72.9 %all-gather.3.cloned.1.call-start = ((), (), s32[]{:S(2)}) async-start(), calls=%async_computation | async-start | bytes 2654208 | tf_op jit(solution)/shard_map/all_gather | solution.py:343
  20.4 40.9 %copy-start.1 = (bf16[48,512]{1,0:T(8,128)(2,1)S(1)}, bf16[48,512]{1,0:T(8,128)(2,1)}, u32[]{:S(2)}) copy-start(bf16[48,512]{1,0:T(8,128)(2,1)} %shard_map.67) | copy-start | bytes 147460
  20.4 5.3 %collective-permute-start = (bf16[1,48,512]{2,1,0:T(8,128)(2,1)}, bf16[1,48,512]{2,1,0:T(8,128)(2,1)S(1)}, u32[]{:S(2)}, u32[]{:S(2)}) collective-permute-start(bf16[1,48,512]{2,1,0:T(8,128)(2,1)} %bitcast.10), channel_id=1, source_target_pairs={{0,4},{4,0},{8,12},{12,8},{16,20},{20,16},{24,28},{28,24},{1,5},{5... | collective-permute-start | bytes 147464 | tf_op jit(solution)/shard_map/ppermute | solution.py:325
  22.9 7.3 %collective-permute-start.4 = (bf16[32,1792]{1,0:T(8,128)(2,1)S(1)}, bf16[32,1792]{1,0:T(8,128)(2,1)S(1)}, u32[]{:S(2)}, u32[]{:S(2)}) collective-permute-start(bf16[32,1792]{1,0:T(8,128)(2,1)S(1)} %get-tuple-element.14), channel_id=1, source_target_pairs={{0,4},{1,12},{2,20},{3,28},{4,0},{5,8},{6,16},{7,24},{8,5},{9,13},... | collective-permute-start | bytes 344072 | tf_op jit(solution)/shard_map/ppermute | solution.py:356
  23.4 6.7 %collective-permute-start.3 = (bf16[32,1792]{1,0:T(8,128)(2,1)S(1)}, bf16[32,1792]{1,0:T(8,128)(2,1)S(1)}, u32[]{:S(2)}, u32[]{:S(2)}) collective-permute-start(bf16[32,1792]{1,0:T(8,128)(2,1)S(1)} %get-tuple-element.15), channel_id=1, source_target_pairs={{0,0},{1,8},{2,16},{3,24},{4,4},{5,12},{6,20},{7,28},{8,1},{9,9},{... | collective-permute-start | bytes 344072 | tf_op jit(solution)/shard_map/ppermute | solution.py:356
  26.4 14.8 %collective-permute-start.1 = (bf16[2,48,512]{2,1,0:T(8,128)(2,1)S(1)}, bf16[2,48,512]{2,1,0:T(8,128)(2,1)S(1)}, u32[]{:S(2)}, u32[]{:S(2)}) collective-permute-start(bf16[2,48,512]{2,1,0:T(8,128)(2,1)S(1)} %pad_maximum_fusion.4), channel_id=1, source_target_pairs={{0,8},{4,12},{8,0},{12,4},{16,24},{20,28},{24,16},{28,20},{1,9},{5... | collective-permute-start | bytes 294920 | tf_op jit(solution)/shard_map/ppermute | solution.py:325
  42.1 19.2 %collective-permute-start.2 = (bf16[4,48,512]{2,1,0:T(8,128)(2,1)S(1)}, bf16[4,48,512]{2,1,0:T(8,128)(2,1)S(1)}, u32[]{:S(2)}, u32[]{:S(2)}) collective-permute-start(bf16[4,48,512]{2,1,0:T(8,128)(2,1)S(1)} %pad_maximum_fusion.3), channel_id=1, source_target_pairs={{0,16},{4,20},{8,24},{12,28},{16,0},{20,4},{24,8},{28,12},{1,17},{... | collective-permute-start | bytes 589832 | tf_op jit(solution)/shard_map/ppermute | solution.py:325
  80.1 1.7 %copy-start = (bf16[256,4608]{1,0:T(8,128)(2,1)S(1)}, bf16[256,4608]{1,0:T(8,128)(2,1)}, u32[]{:S(2)}) copy-start(bf16[256,4608]{1,0:T(8,128)(2,1)} %all-gather.3.cloned.1.call-done.right_ref) | copy-start | bytes 7077892
Sparse Core Ops, SparseCore 0:
  10.8 62.5 all-gather.2
where the time goes:
time: 113 us; the launch traced here: 112 us
  Pallas kernels  45.6 us (40%)
  blocking collectives  18.3 us (16%)
  waiting for transfers between devices  18.2 us (16%)
  between operations  14.8 us (13%)
  starting transfers between devices  9.21 us (8%)
  other arithmetic  3.56 us (3%)
  local copies, waits for them, and re-layouts  2.65 us (2%)
    pallas_call x1, Pallas kernels, on_device(): pl.pallas_call(functools.partial(tile_kernel, (band, col_units, steps)),...  23.7 us
    pallas_call x1, Pallas kernels, on_device(): pl.pallas_call(functools.partial(eliminate_kernel, total_units), out_shap...  18.7 us
    ppermute x3, waiting for transfers between devices, double_up(): block = jnp.concatenate([block, lax.ppermute(block, axis, pairs)], axis=0)  17.7 us
    all_gather x1, blocking collectives, on_device(): lax.all_gather(jnp.concatenate(ordered, axis=0), 'col', axis=0, tiled=True)  10.1 us
    all_gather x1, blocking collectives, on_device(): lax.all_gather(packed, 'col', axis=0)  8.21 us
    ppermute x3, starting transfers between devices, double_up(): block = jnp.concatenate([block, lax.ppermute(block, axis, pairs)], axis=0)  7.95 us
  transfers between devices with their start and end apart: 6, of which 4 were waited for; matrix products, arithmetic and copies ran while one was open for 3% of the time, Pallas kernels for 20%

commit v1 on v0

v1 whole, which is shorter than its diff:
```python
import functools
import jax
import jax.numpy as jnp
from jax import lax
from jax.experimental import pallas as pl
from jax.experimental.pallas import tpu as pltpu
from jax.sharding import PartitionSpec as P

PANEL = 256
CHUNK = 128
GROUP = 64
SLOTS = 3
EXACT = lax.Precision.HIGHEST
VMEM = pl.BlockSpec(memory_space=pltpu.VMEM)
SMEM = pl.BlockSpec(memory_space=pltpu.SMEM)
ANY = pl.BlockSpec(memory_space=pl.ANY)


def iota(shape, dim):
    return lax.broadcasted_iota(jnp.int32, shape, dim)


def product(left_side, right_side, left_dim, right_dim, precision=None):
    return lax.dot_general(
        left_side,
        right_side,
        (((left_dim,), (right_dim,)), ((), ())),
        precision=precision,
        preferred_element_type=jnp.float32,
    )


def split_three(value):
    high = value.astype(jnp.bfloat16)
    rest = value - high.astype(jnp.float32)
    middle = rest.astype(jnp.bfloat16)
    low = (rest - middle.astype(jnp.float32)).astype(jnp.bfloat16)
    return high, middle, low


def store_sums(out_ref, top, sums):
    high, middle, low = (term.astype(jnp.float32) for term in split_three(sums))
    upper = jnp.concatenate([high, middle], axis=1)
    lower = jnp.concatenate([low, jnp.zeros_like(low)], axis=1)
    out_ref[top : top + 16, 0:256] = jnp.concatenate([upper, lower], axis=0).astype(jnp.bfloat16)


def load_sums(rows):
    wide = rows.astype(jnp.float32)
    return wide[0:8, 0:128] + wide[0:8, 128:256] + wide[8:16, 0:128]


def pack_kernel(band, keys_ref, shifts_ref, packed_ref, rights_ref, *piece_refs):
    rows, units = keys_ref.shape
    row_units = units // band
    packed_ref[0:rows, :] = keys_ref[:, 0:PANEL]
    sums = jnp.zeros((8, 128), jnp.float32)
    for lane in range(0, units, 128):
        wide = keys_ref[:, lane : lane + 128].astype(jnp.float32)
        squares = wide * wide
        for top in range(0, rows, 8):
            sums = sums + squares[top : top + 8]
    store_sums(packed_ref, rows, sums)
    rights_ref[:, 0:units] = keys_ref[...]
    rights_ref[:, units:] = shifts_ref[...]
    for turn in range(band):
        for part in range(band):

            @pl.when(lax.rem(lax.axis_index("row") + turn, band) == part)
            def _():
                piece_refs[turn][...] = keys_ref[:, part * row_units : (part + 1) * row_units]


def add_kernel(one_ref, other_ref, out_ref):
    store_sums(out_ref, 0, load_sums(one_ref[...]) + load_sums(other_ref[...]))


def factor_group(tiles, base):
    lane = iota((8, 128), 1)
    sub = iota((8, 128), 0)
    diagonals = []
    for top in range(len(tiles)):
        live = range(top, len(tiles))
        first = base + 8 * top
        columns = [
            {at: jnp.broadcast_to(tiles[at][:, first + q : first + q + 1], (8, 128)) for at in live}
            for q in range(8)
        ]
        scale = jnp.zeros((8, 128), jnp.float32)
        pivots = jnp.zeros((8, 128), jnp.float32)
        for q in range(8):
            column = columns[q]
            pivot = jnp.broadcast_to(column[top][q : q + 1, :], (8, 128))
            inverse = 1.0 / pivot
            for k in range(q + 1, 8):
                factor = jnp.broadcast_to(column[top][k : k + 1, :], (8, 128)) * inverse
                for at in live:
                    columns[k][at] = columns[k][at] - column[at] * factor
            row = jnp.broadcast_to(tiles[top][q : q + 1, :], (8, 128))
            row = jnp.where(lane == first + q, 1.0, row)
            scaled = row * inverse
            for at in live:
                kept = jnp.where(lane == first + q, 0.0, tiles[at])
                new = kept - column[at] * scaled
                if at == top:
                    new = jnp.where(sub < q, tiles[at], jnp.where(sub == q, row, new))
                tiles[at] = new
            scale = jnp.where(sub == q, lax.rsqrt(pivot), scale)
            pivots = jnp.where(sub == q, pivot, pivots)
        tiles[top] = tiles[top] * scale
        diagonals.append(pivots * scale)
    return tiles, diagonals


def factor_chunk(work):
    lane = iota((CHUNK, CHUNK), 1)
    row = iota((CHUNK, CHUNK), 0)
    diagonals = []
    for base in range(0, CHUNK, GROUP):
        rest = base + GROUP
        tiles = [work[top : top + 8, :] for top in range(base, rest, 8)]
        tiles, found = factor_group(tiles, base)
        diagonals += found
        done = jnp.concatenate(tiles, axis=0)
        work[base:rest, :] = done
        if rest < CHUNK:
            group_lane = lane[base:rest]
            upper = (group_lane > row[base:rest]) & (group_lane < rest)
            update = product(done, jnp.where(upper, 0.0, done), 0, 0, EXACT)[rest:]
            later_lane = lane[rest:]
            own = (later_lane >= base) & (later_lane < rest)
            work[rest:, :] = jnp.where(own, 0.0, work[rest:, :]) - update
    both = work[...]
    diagonal = jnp.concatenate(diagonals, axis=0)
    inverse = jnp.where(lane <= row, both, 0.0)
    factor = jnp.where(lane > row, both, jnp.where(lane == row, diagonal, 0.0))
    return inverse, factor


def snake_place(row, row_count, band):
    lines = row_count // band
    line, place = row // band, lax.rem(row, band)
    back = lines - 1 - line
    inner = jnp.where(lax.rem(back, 2) == 0, place - 1, band - 1 - place)
    return jnp.where(place == 0, line, lines + back * (band - 1) + inner)


def eliminate_panel(rows, carried, ridge, work):
    solved = []
    factors = []
    for chunk, row in enumerate(rows):
        low, high = chunk * CHUNK, (chunk + 1) * CHUNK
        block = row[:, low:high] + ridge
        for done in carried + solved:
            block = block - product(done[:, low:high], done[:, low:high], 0, 0, EXACT)
        work[chunk] = block
        later = row[:, high:]
        for done in carried + solved:
            later = later - product(done[:, low:high], done[:, high:], 0, 0, EXACT)
        inverse, factor = factor_chunk(work.at[chunk])
        later = product(inverse, later, 1, 0, EXACT)
        solved.append(jnp.concatenate([jnp.zeros((CHUNK, high), jnp.float32), later], axis=1))
        factors.append(factor)
    square = jnp.zeros((CHUNK, CHUNK), jnp.float32)
    upper = jnp.concatenate([factors[0], solved[0][:, CHUNK : 2 * CHUNK]], axis=1)
    under = jnp.concatenate([square, factors[1]], axis=1)
    return solved, jnp.concatenate([upper, under], axis=0).T


def put_vectors(solved, middle, vectors_ref, heads_ref):
    depth = vectors_ref.shape[0]
    for chunk, row in enumerate(solved):
        low, high = chunk * CHUNK, (chunk + 1) * CHUNK
        vector = row[:, -depth:]
        vectors_ref[:, low:high] = vector.T
        first, second, _ = split_three(vector)
        heads_ref[low:high, 0:depth] = first
        heads_ref[low:high, depth : 2 * depth] = second
        middle = middle - product(vector, vector, 0, 0, EXACT)
    return middle


def ridge_of(amount):
    square = (CHUNK, CHUNK)
    near = iota(square, 0) == iota(square, 1)
    return jnp.where(near, jnp.broadcast_to(amount, square), 0.0)


def first_kernel(
    total_units,
    masks,
    band,
    ridge_ref,
    near_ref,
    far_ref,
    near_mate_ref,
    far_mate_ref,
    amount_ref,
    lower_ref,
    vectors_ref,
    heads_ref,
    carried_ref,
    middle_ref,
    keys_ref,
    staged,
    keys,
    work,
):
    half = near_ref.shape[0]
    rows = near_ref.shape[1] - 32
    row_index = lax.axis_index("row")
    parity = lax.rem(lax.axis_index("col"), 2)
    sums = jnp.zeros((8, 128), jnp.float32)
    for panel, pair in ((parity, (near_ref, far_ref)), (1 - parity, (near_mate_ref, far_mate_ref))):
        for place, source in enumerate(pair):
            for shard in range(half):
                at = snake_place(row_index ^ (masks[shard] + place), 2 * half, band)
                staged[panel, at] = source[shard, 0:rows, :]
                sums = sums + load_sums(source[shard, rows : rows + 16, :])
                sums = sums + load_sums(source[shard, rows + 16 : rows + 32, :])
    for shard in range(2 * half):
        for panel in range(2):
            top, lane = shard * rows, panel * PANEL
            keys[top : top + rows, lane : lane + PANEL] = staged[panel, shard]
    total = jnp.sum(jnp.sum(sums, axis=0, keepdims=True), axis=1, keepdims=True)
    amount = total * ridge_ref[0] / total_units
    amount_ref[...] = jnp.broadcast_to(amount, amount_ref.shape)
    held = keys[...]
    depth = held.shape[0]
    keys_ref[...] = held[:, PANEL:]
    gram = product(held[:, :PANEL], held, 0, 0)
    whole = jnp.concatenate([gram, held[:, :PANEL].astype(jnp.float32).T], axis=1)
    chunks = [whole[low : low + CHUNK] for low in range(0, PANEL, CHUNK)]
    solved, lower = eliminate_panel(chunks, [], ridge_of(amount), work)
    lower_ref[...] = lower
    for chunk, row in enumerate(solved):
        carried_ref[chunk] = row[:, PANEL:]
    middle = jnp.where(iota((depth, depth), 0) == iota((depth, depth), 1), 1.0, 0.0)
    middle_ref[...] = put_vectors(solved, middle, vectors_ref, heads_ref)


def second_kernel(
    amount_ref,
    carried_ref,
    middle_ref,
    keys_ref,
    lower_ref,
    vectors_ref,
    heads_ref,
    terms_ref,
    work,
):
    held = keys_ref[...]
    gram = product(held, held, 0, 0)
    whole = jnp.concatenate([gram, held.astype(jnp.float32).T], axis=1)
    chunks = [whole[low : low + CHUNK] for low in range(0, PANEL, CHUNK)]
    carried = [carried_ref[chunk] for chunk in range(PANEL // CHUNK)]
    solved, lower = eliminate_panel(chunks, carried, ridge_of(amount_ref[0:1, 0:1]), work)
    lower_ref[...] = lower
    middle = put_vectors(solved, middle_ref[...], vectors_ref, heads_ref)
    for place, term in enumerate(split_three(middle)):
        terms_ref[place] = term


def tile_kernel(
    sizes,
    amount_ref,
    terms_ref,
    heads_a_ref,
    heads_b_ref,
    vectors_a_ref,
    vectors_b_ref,
    lower_a_ref,
    lower_b_ref,
    rights_ref,
    *refs,
):
    band, col_units = sizes
    row_refs, refs = refs[:-11], refs[-11:]
    panel_a_ref, panel_b_ref, trailing_ref, forward_ref, *refs = refs
    blocks, right, out, staged, left, block_sems, out_sems = refs
    count, depth, width = blocks.shape
    row_units = left.shape[0]
    col_count = col_units // width
    row_index = lax.axis_index("row")
    col_index = lax.axis_index("col")
    in_a = row_index == 0
    in_b = row_index == band
    loads = [
        pltpu.make_async_copy(
            rights_ref.at[:, step * width : (step + 1) * width], blocks.at[step], block_sems.at[step]
        )
        for step in range(count)
    ]
    for load in loads:
        load.start()
    row_count, rows = staged.shape[0:2]
    part = lax.rem(row_index, band)
    for mask, source in enumerate(row_refs):
        for turn in range(band):
            row = (col_index ^ mask) * band + lax.rem(part - turn + band, band)
            staged[snake_place(row, row_count, band)] = source[turn]
    held = jnp.concatenate([staged[shard] for shard in range(row_count)], axis=0)
    flipped = held.astype(jnp.float32).T.astype(jnp.bfloat16)
    left[:, 0:depth] = flipped
    left[:, depth:] = flipped

    def put_right(step):
        if step < count:
            loads[step].wait()
            block = blocks[step]
            value = product(terms_ref[2], block, 1, 0) + product(terms_ref[1], block, 1, 0)
            value = value + product(terms_ref[0], block, 1, 0)
        else:
            first = (step - count) * width
            parts = (vectors_a_ref, vectors_b_ref)[first // PANEL : (first + width) // PANEL]
            value = jnp.concatenate([ref[...] for ref in parts], axis=1)
        high = value.astype(jnp.bfloat16)
        right[step % 2, 0:depth, :] = high
        right[step % 2, depth:, :] = (value - high.astype(jnp.float32)).astype(jnp.bfloat16)

    def copies(step):
        slot = step % SLOTS
        if step < count:
            target, at = trailing_ref, step * width
            if step >= col_count:
                target, at = forward_ref, (step - col_count) * width
            target = target.at[:, at : at + width]
            return [pltpu.make_async_copy(out.at[slot], target, out_sems.at[slot, 0])]
        first = (step - count) * width
        return [
            pltpu.make_async_copy(
                out.at[slot, :, lane : lane + PANEL],
                (panel_a_ref, panel_b_ref)[(first + lane) // PANEL],
                out_sems.at[slot, lane // PANEL],
            )
            for lane in range(0, width, PANEL)
        ]

    def finish_trailing(step, slot):
        apart = col_index * col_units + step * width - row_index * row_units

        amount = jnp.broadcast_to(amount_ref[0:1, 0:1], (64, 128))

        def add_ridge(piece, carry):
            top = pl.multiple_of(piece * 64, 64)
            lane = pl.multiple_of((top - apart) // 128 * 128, 128)
            near = iota((64, 128), 0) + (top - apart - lane) == iota((64, 128), 1)
            held = out[slot, pl.ds(top, 64), pl.ds(lane, 128)]
            out[slot, pl.ds(top, 64), pl.ds(lane, 128)] = held + jnp.where(near, amount, 0.0)
            return carry

        first = jnp.clip(apart, 0, row_units) // 64
        lax.fori_loop(first, jnp.clip(apart + width, 0, row_units) // 64, add_ridge, 0)

        @pl.when(in_a | in_b)
        def _():
            out[slot, 0:PANEL, :] = jnp.zeros((PANEL, width), jnp.float32)

        if step == 0:

            @pl.when(col_index < 2)
            def _():
                out[slot, :, 0:PANEL] = jnp.zeros((row_units, PANEL), jnp.float32)

    def finish_forward(step, slot):
        for here, heads in ((in_a, heads_a_ref), (in_b, heads_b_ref)):

            @pl.when(here)
            def _():
                block = blocks[step]
                out[slot, 0:PANEL, :] = product(heads[:, 0:depth], block, 1, 0) + product(
                    heads[:, depth:], block, 1, 0
                )

    def finish_panels(step, slot):
        for lane in range(0, width, PANEL):
            panel = ((step - count) * width + lane) // PANEL

            @pl.when(in_a)
            def _():
                block = jnp.zeros((PANEL, PANEL), jnp.float32)
                out[slot, 0:PANEL, lane : lane + PANEL] = block if panel else lower_a_ref[...]

            if panel:

                @pl.when(in_b)
                def _():
                    out[slot, 0:PANEL, lane : lane + PANEL] = lower_b_ref[...]

    steps = count + 2 * PANEL // width
    put_right(0)
    for step in range(steps):
        slot = step % SLOTS
        if step >= SLOTS:
            for copy in copies(step - SLOTS):
                copy.wait()
        if step + 1 < steps:
            put_right(step + 1)
        out[slot] = product(left[...], right[step % 2], 1, 0)
        if step < col_count:
            finish_trailing(step, slot)
        elif step < count:
            finish_forward(step, slot)
        else:
            finish_panels(step, slot)
        for copy in copies(step):
            copy.start()
    for step in range(steps - SLOTS, steps):
        for copy in copies(step):
            copy.wait()


def snake(row_count, band):
    lines = row_count // band
    order = [line * band for line in range(lines)]
    for line in reversed(range(lines)):
        places = [line * band + place for place in range(1, band)]
        order += places if (lines - 1 - line) % 2 == 0 else places[::-1]
    return order


def exchange(block, axis, count, step):
    return lax.ppermute(block, axis, [(place, place ^ step) for place in range(count)])


def on_device(edit_keys, edit_shifts, ridge_scale):
    row_count = lax.axis_size("row")
    col_count = lax.axis_size("col")
    rows, col_units = edit_keys.shape
    shift_cols = edit_shifts.shape[1]
    depth = rows * row_count
    total_units = col_units * col_count
    row_units = total_units // row_count
    band = row_count // col_count

    packed, shares, *pieces = pl.pallas_call(
        functools.partial(pack_kernel, band),
        out_shape=(
            jax.ShapeDtypeStruct((rows + 16, PANEL), jnp.bfloat16),
            jax.ShapeDtypeStruct((rows, col_units + shift_cols), jnp.bfloat16),
        )
        + (jax.ShapeDtypeStruct((rows, row_units), jnp.bfloat16),) * band,
        in_specs=[VMEM, VMEM],
        out_specs=(VMEM,) * (2 + band),
    )(edit_keys, edit_shifts)
    moved = []
    for turn in range(band):
        pairs = []
        for row in range(row_count):
            for col in range(col_count):
                target = (col * band + (row + turn) % band) * col_count + row // band
                pairs.append((row * col_count + col, target))
        moved.append(lax.ppermute(pieces[turn], ("row", "col"), pairs))
    near, sums = packed[:rows], packed[rows:]
    bit = col_count // 2
    while bit > 1:
        other = exchange(packed, "col", col_count, bit)
        low = (lax.axis_index("col") // bit) % 2 == 0
        near = jnp.where(low, packed[:rows], other[:rows])
        sums = [packed[rows:], other[rows:]]
        bit //= 2
        if bit > 1:
            sums = pl.pallas_call(
                add_kernel,
                out_shape=jax.ShapeDtypeStruct((16, PANEL), jnp.bfloat16),
                in_specs=[VMEM, VMEM],
                out_specs=VMEM,
            )(*sums)
            packed = jnp.concatenate([near, sums], axis=0)
    near = jnp.concatenate([near] + sums, axis=0)[None]
    order = snake(row_count, band)
    rights = lax.all_gather(shares, "row", axis=0, tiled=True, axis_index_groups=[order])
    masks = [0]
    bit = row_count // 2
    while bit > 1:
        near = jnp.concatenate([near, exchange(near, "row", row_count, bit)], axis=0)
        masks += [held + bit for held in masks]
        bit //= 2
    far = exchange(near, "row", row_count, 1)
    near_mate = exchange(near, "col", col_count, 1)
    far_mate = exchange(far, "col", col_count, 1)

    part = functools.partial(jax.ShapeDtypeStruct, dtype=jnp.float32)
    part_low = functools.partial(jax.ShapeDtypeStruct, dtype=jnp.bfloat16)
    cost = pl.CostEstimate(flops=10**10, bytes_accessed=10**6, transcendentals=0)
    amount, lower_a, vectors_a, heads_a, carried, middle, keys_b = pl.pallas_call(
        functools.partial(first_kernel, total_units, masks, band),
        out_shape=(
            part((8, 128)),
            part((PANEL, PANEL)),
            part((depth, PANEL)),
            part_low((PANEL, 2 * depth)),
            part((PANEL // CHUNK, CHUNK, PANEL + depth)),
            part((depth, depth)),
            part_low((depth, PANEL)),
        ),
        in_specs=[SMEM] + [VMEM] * 4,
        out_specs=(VMEM,) * 7,
        scratch_shapes=[
            pltpu.VMEM((2, row_count, rows, PANEL), jnp.bfloat16),
            pltpu.VMEM((depth, 2 * PANEL), jnp.bfloat16),
            pltpu.VMEM((PANEL // CHUNK, CHUNK, CHUNK), jnp.float32),
        ],
        compiler_params=pltpu.CompilerParams(vmem_limit_bytes=32 * 2**20),
        cost_estimate=cost,
    )(ridge_scale, near, far, near_mate, far_mate)
    moved, amount = lax.optimization_barrier((moved, amount))
    row_keys = [jnp.stack(moved)]
    for mask in range(1, col_count):
        row_keys.append(exchange(row_keys[0], "col", col_count, mask))
    lower_b, vectors_b, heads_b, terms = pl.pallas_call(
        second_kernel,
        out_shape=(
            part((PANEL, PANEL)),
            part((depth, PANEL)),
            part_low((PANEL, 2 * depth)),
            part_low((3, depth, depth)),
        ),
        in_specs=[VMEM] * 4,
        out_specs=(VMEM,) * 4,
        scratch_shapes=[
            pltpu.VMEM((PANEL // CHUNK, CHUNK, CHUNK), jnp.float32),
        ],
        compiler_params=pltpu.CompilerParams(vmem_limit_bytes=32 * 2**20),
        cost_estimate=cost,
    )(amount, carried, middle, keys_b)

    width = 2 * PANEL
    if col_units % width or shift_cols % width:
        width = PANEL
    count = (col_units + shift_cols) // width
    return tuple(
        pl.pallas_call(
            functools.partial(tile_kernel, (band, col_units)),
            out_shape=(
                jax.ShapeDtypeStruct((row_units, PANEL), jnp.float32),
                jax.ShapeDtypeStruct((row_units, PANEL), jnp.float32),
                jax.ShapeDtypeStruct((row_units, col_units), jnp.float32),
                jax.ShapeDtypeStruct((row_units, shift_cols), jnp.float32),
            ),
            in_specs=[VMEM] * 8 + [ANY] + [VMEM] * col_count,
            out_specs=(ANY, ANY, ANY, ANY),
            scratch_shapes=[
                pltpu.VMEM((count, depth, width), jnp.bfloat16),
                pltpu.VMEM((2, 2 * depth, width), jnp.bfloat16),
                pltpu.VMEM((SLOTS, row_units, width), jnp.float32),
                pltpu.VMEM((row_count, rows, row_units), jnp.bfloat16),
                pltpu.VMEM((row_units, 2 * depth), jnp.bfloat16),
                pltpu.SemaphoreType.DMA((count,)),
                pltpu.SemaphoreType.DMA((SLOTS, 2)),
            ],
            compiler_params=pltpu.CompilerParams(vmem_limit_bytes=40 * 2**20),
            cost_estimate=pl.CostEstimate(
                flops=10**10, bytes_accessed=4 * 10**7, transcendentals=0
            ),
        )(
            amount,
            terms,
            heads_a,
            heads_b,
            vectors_a,
            vectors_b,
            lower_a,
            lower_b,
            rights,
            *row_keys,
        )
    )


def solution(mesh):
    return jax.shard_map(
        on_device,
        mesh=mesh,
        in_specs=(P("row", "col"), P("row", "col"), P()),
        out_specs=(P("row", None), P("row", None), P("row", "col"), P("row", "col")),
        check_vma=False,
    )
```

time: 113 us -> 92.5 us (0.82)
  blocking collectives: 18.3 us -> 0 us
  starting transfers between devices: 9.21 us -> 23.7 us
  Pallas kernels: 45.6 us -> 37.7 us
  waiting for transfers between devices: 18.2 us -> 12.8 us
  other arithmetic: 3.56 us -> 0.78 us
    all_gather x2 -> x0, blocking collectives: 18.3 us -> none  [the longest x1 10.1 us: on_device(): lax.all_gather(jnp.concatenate(ordered, axis=0), 'col', axis=0, tiled=True)]
    ppermute x5 -> x11, starting transfers between devices: 9.17 us -> 23.7 us  [the longest x9 20.4 us: exchange(): lax.ppermute(block, axis, [(place, place ^ step) for place in range(count)])]
    pallas_call x4, Pallas kernels: 45.6 us -> 37.7 us  [the longest x1 17.1 us: on_device(): pl.pallas_call(functools.partial(tile_kernel, (band, col_units)), out_sha...]
    ppermute x5 -> x11, waiting for transfers between devices: 18.1 us -> 12.8 us  [the longest x9 12.7 us: exchange(): lax.ppermute(block, axis, [(place, place ^ step) for place in range(count)])]
    concatenate x5 -> x2, other arithmetic: 3.4 us -> 0.02 us  [on_device(): jnp.concatenate([near, exchange(near, 'row', row_count, bit)], axis=0)]
  transfers between devices with their start and end apart: 6 -> 12, of which waited for: 4 -> 4; matrix products, arithmetic and copies ran while one was open for 3% -> 2% of each run, Pallas kernels for 20% -> 20%
where the time goes in v1:
time: 92.5 us; the launch traced here: 92.2 us
  Pallas kernels  37.7 us (41%)
  starting transfers between devices  23.7 us (26%)
  between operations  14.8 us (16%)
  waiting for transfers between devices  12.8 us (14%)
  local copies, waits for them, and re-layouts  2.39 us (3%)
    ppermute x9, starting transfers between devices, exchange(): lax.ppermute(block, axis, [(place, place ^ step) for place in range(count)])  20.4 us
    pallas_call x1, Pallas kernels, on_device(): pl.pallas_call(functools.partial(tile_kernel, (band, col_units)), out_sha...  17.1 us
    ppermute x9, waiting for transfers between devices, exchange(): lax.ppermute(block, axis, [(place, place ^ step) for place in range(count)])  12.7 us
    pallas_call x1, Pallas kernels, on_device(): pl.pallas_call(second_kernel, out_shape=(part((PANEL, PANEL)), part((dept...  9.47 us
    pallas_call x1, Pallas kernels, on_device(): pl.pallas_call(functools.partial(first_kernel, total_units, masks, band),...  9.24 us
    ppermute x2, starting transfers between devices, on_device(): moved.append(lax.ppermute(pieces[turn], ('row', 'col'), pairs))  3.26 us
    pallas_call x1, Pallas kernels, on_device(): pl.pallas_call(functools.partial(pack_kernel, band), out_shape=(jax.Shape...  1.88 us
  transfers between devices with their start and end apart: 12, of which 4 were waited for; matrix products, arithmetic and copies ran while one was open for 2% of the time, Pallas kernels for 20%

profile of v1, /device:TPU:0, one launch (start us, length us, event | category | flops | bytes accessed | tf_op | source)
XLA Modules:
  0.0 92.2 jit_solution(17907831289039814828)
XLA Ops:
  7.2 0.0 all-gather.2.cloned.1.call-start
  7.2 1.9 %shard_map.66 = (bf16[48,256]{1,0:T(8,128)(2,1)}, bf16[32,4608]{1,0:T(8,128)(2,1)}, bf16[32,1792]{1,0:T(8,128)(2,1)}, bf16[32,1792]{1,0:T(8,128)(2,1)}) custom-call(bf16[32,3584]{1,0:T(8,128)(2,1)} %keys_ref.1, bf16[32,1024]{1,0:T(8,128)(2,1)} %shifts_ref.1), custom_call_target="tpu_custom_call" | custom-call | tf_op jit(solution)/shard_map/pallas_call | solution.py:437
  9.1 0.0 all-gather.2.cloned.1.call-update
  9.1 3.0 %collective-permute-start.2 = (bf16[48,256]{1,0:T(8,128)(2,1)}, bf16[48,256]{1,0:T(8,128)(2,1)S(1)}, u32[]{:S(2)}, u32[]{:S(2)}) collective-permute-start(bf16[48,256]{1,0:T(8,128)(2,1)} %get-tuple-element.24), channel_id=1, source_target_pairs={{0,2},{1,3},{2,0},{3,1},{4,6},{5,7},{6,4},{7,5},{8,10},{9,11},{10,... | collective-permute-start | bytes 73736 | tf_op jit(solution)/shard_map/ppermute | solution.py:424
  12.1 0.7 slice.14
  12.9 1.3 %collective-permute-done.2 = bf16[48,256]{1,0:T(8,128)(2,1)S(1)} collective-permute-done((bf16[48,256]{1,0:T(8,128)(2,1)}, bf16[48,256]{1,0:T(8,128)(2,1)S(1)}, u32[]{:S(2)}, u32[]{:S(2)}) %collective-permute-start.2) | collective-permute-done | bytes 24608 | tf_op jit(solution)/shard_map/ppermute | solution.py:424
  14.1 0.7 slice_select_fusion
  14.9 3.1 %collective-permute-start.3 = (bf16[1,64,256]{2,1,0:T(8,128)(2,1)S(1)}, bf16[1,64,256]{2,1,0:T(8,128)(2,1)S(1)}, u32[]{:S(2)}, u32[]{:S(2)}) collective-permute-start(bf16[1,64,256]{2,1,0:T(8,128)(2,1)S(1)} %maximum_bitcast_fusion), channel_id=1, source_target_pairs={{0,16},{4,20},{8,24},{12,28},{16,0},{20,4},{24,8},{28,12},{1,17},{... | collective-permute-start | bytes 98312 | tf_op jit(solution)/shard_map/ppermute | solution.py:424
  18.0 2.0 %collective-permute-done.3 = bf16[1,64,256]{2,1,0:T(8,128)(2,1)S(1)} collective-permute-done((bf16[1,64,256]{2,1,0:T(8,128)(2,1)S(1)}, bf16[1,64,256]{2,1,0:T(8,128)(2,1)S(1)}, u32[]{:S(2)}, u32[]{:S(2)}) %collective-permute-start.3) | collective-permute-done | bytes 32800 | tf_op jit(solution)/shard_map/ppermute | solution.py:424
  20.0 1.9 %collective-permute-start.4 = (bf16[2,64,256]{2,1,0:T(8,128)(2,1)S(1)}, bf16[2,64,256]{2,1,0:T(8,128)(2,1)S(1)}, u32[]{:S(2)}, u32[]{:S(2)}) collective-permute-start(bf16[2,64,256]{2,1,0:T(8,128)(2,1)S(1)} %pad_maximum_fusion.2), channel_id=1, source_target_pairs={{0,8},{4,12},{8,0},{12,4},{16,24},{20,28},{24,16},{28,20},{1,9},{5... | collective-permute-start | bytes 196616 | tf_op jit(solution)/shard_map/ppermute | solution.py:424
  21.9 3.5 %collective-permute-done.4 = bf16[2,64,256]{2,1,0:T(8,128)(2,1)S(1)} collective-permute-done((bf16[2,64,256]{2,1,0:T(8,128)(2,1)S(1)}, bf16[2,64,256]{2,1,0:T(8,128)(2,1)S(1)}, u32[]{:S(2)}, u32[]{:S(2)}) %collective-permute-start.4) | collective-permute-done | bytes 65568 | tf_op jit(solution)/shard_map/ppermute | solution.py:424
  25.4 1.9 %collective-permute-start.5 = (bf16[4,64,256]{2,1,0:T(8,128)(2,1)S(1)}, bf16[4,64,256]{2,1,0:T(8,128)(2,1)S(1)}, u32[]{:S(2)}, u32[]{:S(2)}) collective-permute-start(bf16[4,64,256]{2,1,0:T(8,128)(2,1)S(1)} %pad_maximum_fusion.1.near_ref), channel_id=1, source_target_pairs={{0,4},{4,0},{8,12},{12,8},{16,20},{20,16},{24,28},{28,24},{1,5},{5... | collective-permute-start | bytes 393224 | tf_op jit(solution)/shard_map/ppermute | solution.py:424
  27.3 0.0 collective-permute-start.6
  27.3 5.9 %collective-permute-done.5.far_ref = bf16[4,64,256]{2,1,0:T(8,128)(2,1)S(1)} collective-permute-done((bf16[4,64,256]{2,1,0:T(8,128)(2,1)S(1)}, bf16[4,64,256]{2,1,0:T(8,128)(2,1)S(1)}, u32[]{:S(2)}, u32[]{:S(2)}) %collective-permute-start.5) | collective-permute-done | bytes 131104 | tf_op jit(solution)/shard_map/ppermute | solution.py:424
  33.2 0.0 collective-permute-start.7
  33.2 1.5 %collective-permute-start = (bf16[32,1792]{1,0:T(8,128)(2,1)}, bf16[32,1792]{1,0:T(8,128)(2,1)S(1)}, u32[]{:S(2)}, u32[]{:S(2)}) collective-permute-start(bf16[32,1792]{1,0:T(8,128)(2,1)} %get-tuple-element.22), channel_id=1, source_target_pairs={{0,0},{1,8},{2,16},{3,24},{4,4},{5,12},{6,20},{7,28},{8,1},{9,9},{... | collective-permute-start | bytes 344072 | tf_op jit(solution)/shard_map/ppermute | solution.py:454
  34.8 1.7 %collective-permute-start.1 = (bf16[32,1792]{1,0:T(8,128)(2,1)}, bf16[32,1792]{1,0:T(8,128)(2,1)S(1)}, u32[]{:S(2)}, u32[]{:S(2)}) collective-permute-start(bf16[32,1792]{1,0:T(8,128)(2,1)} %get-tuple-element.23), channel_id=1, source_target_pairs={{0,4},{1,12},{2,20},{3,28},{4,0},{5,8},{6,16},{7,24},{8,5},{9,13},... | collective-permute-start | bytes 344072 | tf_op jit(solution)/shard_map/ppermute | solution.py:454
  37.1 0.0 collective-permute-done.6.near_mate_ref
  37.2 0.0 collective-permute-done.7.far_mate_ref
  37.2 9.2 %shard_map.67 = (f32[8,128]{1,0:T(8,128)S(1)}, f32[256,256]{1,0:T(8,128)S(1)}, f32[256,256]{1,0:T(8,128)S(1)}, bf16[256,512]{1,0:T(8,128)(2,1)S(1)}, f32[2,128,5...) custom-call(f32[1]{0:T(128)S(6)} %copy.7.ridge_ref, ...), custom_call_target="tpu_custom_call" | custom-call | flops 10000000000 | bytes 1000000 | tf_op jit(solution)/shard_map/pallas_call | solution.py:487
  46.4 0.0 collective-permute-done
  46.4 0.0 collective-permute-done.1
  46.5 6.7 %collective-permute-start.10 = (bf16[2,32,1792]{2,1,0:T(8,128)(2,1)S(1)}, bf16[2,32,1792]{2,1,0:T(8,128)(2,1)S(1)}, u32[]{:S(2)}, u32[]{:S(2)}) collective-permute-start(bf16[2,32,1792]{2,1,0:T(8,128)(2,1)S(1)} %pad_maximum_fusion.refs_0_), channel_id=1, source_target_pairs={{0,3},{1,2},{2,1},{3,0},{4,7},{5,6},{6,5},{7,4},{8,11},{9,10},{10,... | collective-permute-start | bytes 688136 | tf_op jit(solution)/shard_map/ppermute | solution.py:424
  53.2 3.7 %collective-permute-start.9 = (bf16[2,32,1792]{2,1,0:T(8,128)(2,1)S(1)}, bf16[2,32,1792]{2,1,0:T(8,128)(2,1)S(1)}, u32[]{:S(2)}, u32[]{:S(2)}) collective-permute-start(bf16[2,32,1792]{2,1,0:T(8,128)(2,1)S(1)} %pad_maximum_fusion.refs_0_), channel_id=1, source_target_pairs={{0,2},{1,3},{2,0},{3,1},{4,6},{5,7},{6,4},{7,5},{8,10},{9,11},{10,... | collective-permute-start | bytes 688136 | tf_op jit(solution)/shard_map/ppermute | solution.py:424
  56.9 0.0 collective-permute-start.8
  57.0 9.5 %shard_map.68 = (f32[256,256]{1,0:T(8,128)S(1)}, f32[256,256]{1,0:T(8,128)S(1)}, bf16[256,512]{1,0:T(8,128)(2,1)S(1)}, bf16[3,256,256]{2,1,0:T(8,128)(2,1)S(1)}) custom-call(f32[8,128]{1,0:T(8,128)S(1)} %get-tuple-element.26.amount_ref, f32[2,128,512]{2,1,0:T(8,128)S(1)} %get-tuple-element.27.carried_ref, f32[256,256]{1,0:T(8,128)S(1)} %get-tuple-element.28.middle_ref, ...), custom_call_target="tpu_custom_call" | custom-call | flops 10000000000 | bytes 1000000 | tf_op jit(solution)/shard_map/pallas_call | solution.py:512
  66.5 0.0 collective-permute-done.10.refs_3_
  66.5 0.0 collective-permute-done.9.refs_2_
  66.5 0.0 collective-permute-done.8.refs_1_
  66.5 0.0 all-gather.2.cloned.1.call-done.rights_ref
  66.5 1.7 %copy-done = bf16[256,4608]{1,0:T(8,128)(2,1)S(1)} copy-done((bf16[256,4608]{1,0:T(8,128)(2,1)S(1)}, bf16[256,4608]{1,0:T(8,128)(2,1)}, u32[]{:S(2)}) %copy-start) | copy-done | bytes 2359320
  68.2 17.1 %shard_map.69 = (f32[1792,256]{1,0:T(8,128)}, f32[1792,256]{1,0:T(8,128)}, f32[1792,3584]{1,0:T(8,128)}, f32[1792,1024]{1,0:T(8,128)}) custom-call(f32[8,128]{1,0:T(8,128)S(1)} %get-tuple-element.26.amount_ref, bf16[3,256,256]{2,1,0:T(8,128)(2,1)S(1)} %get-tuple-element.30.terms_ref, bf16[256,512]{1,0:T(8,128)(2,1)S(1)} %get-tuple-element.31.heads_a_ref, ...), custom_call_target="tpu_custom_call" | custom-call | flops 10000000000 | bytes 40000000 | tf_op jit(solution)/shard_map/pallas_call | solution.py:534
  (6 shorter events, 0.1 us)
Async XLA Ops:
  7.2 59.4 %all-gather.2.cloned.1.call-start = ((), (), s32[]{:S(2)}) async-start(), calls=%async_computation | async-start | bytes 2654208 | tf_op jit(solution)/shard_map/all_gather | solution.py:473
  9.1 5.0 %collective-permute-start.2 = (bf16[48,256]{1,0:T(8,128)(2,1)}, bf16[48,256]{1,0:T(8,128)(2,1)S(1)}, u32[]{:S(2)}, u32[]{:S(2)}) collective-permute-start(bf16[48,256]{1,0:T(8,128)(2,1)} %get-tuple-element.24), channel_id=1, source_target_pairs={{0,2},{1,3},{2,0},{3,1},{4,6},{5,7},{6,4},{7,5},{8,10},{9,11},{10,... | collective-permute-start | bytes 73736 | tf_op jit(solution)/shard_map/ppermute | solution.py:424
  14.9 5.1 %collective-permute-start.3 = (bf16[1,64,256]{2,1,0:T(8,128)(2,1)S(1)}, bf16[1,64,256]{2,1,0:T(8,128)(2,1)S(1)}, u32[]{:S(2)}, u32[]{:S(2)}) collective-permute-start(bf16[1,64,256]{2,1,0:T(8,128)(2,1)S(1)} %maximum_bitcast_fusion), channel_id=1, source_target_pairs={{0,16},{4,20},{8,24},{12,28},{16,0},{20,4},{24,8},{28,12},{1,17},{... | collective-permute-start | bytes 98312 | tf_op jit(solution)/shard_map/ppermute | solution.py:424
  20.0 5.4 %collective-permute-start.4 = (bf16[2,64,256]{2,1,0:T(8,128)(2,1)S(1)}, bf16[2,64,256]{2,1,0:T(8,128)(2,1)S(1)}, u32[]{:S(2)}, u32[]{:S(2)}) collective-permute-start(bf16[2,64,256]{2,1,0:T(8,128)(2,1)S(1)} %pad_maximum_fusion.2), channel_id=1, source_target_pairs={{0,8},{4,12},{8,0},{12,4},{16,24},{20,28},{24,16},{28,20},{1,9},{5... | collective-permute-start | bytes 196616 | tf_op jit(solution)/shard_map/ppermute | solution.py:424
  25.4 7.8 %collective-permute-start.5 = (bf16[4,64,256]{2,1,0:T(8,128)(2,1)S(1)}, bf16[4,64,256]{2,1,0:T(8,128)(2,1)S(1)}, u32[]{:S(2)}, u32[]{:S(2)}) collective-permute-start(bf16[4,64,256]{2,1,0:T(8,128)(2,1)S(1)} %pad_maximum_fusion.1.near_ref), channel_id=1, source_target_pairs={{0,4},{4,0},{8,12},{12,8},{16,20},{20,16},{24,28},{28,24},{1,5},{5... | collective-permute-start | bytes 393224 | tf_op jit(solution)/shard_map/ppermute | solution.py:424
  27.3 9.9 %collective-permute-start.6 = (bf16[4,64,256]{2,1,0:T(8,128)(2,1)S(1)}, bf16[4,64,256]{2,1,0:T(8,128)(2,1)S(1)}, u32[]{:S(2)}, u32[]{:S(2)}) collective-permute-start(bf16[4,64,256]{2,1,0:T(8,128)(2,1)S(1)} %pad_maximum_fusion.1.near_ref), channel_id=1, source_target_pairs={{0,1},{1,0},{2,3},{3,2},{4,5},{5,4},{6,7},{7,6},{8,9},{9,8},{10,11... | collective-permute-start | bytes 393224 | tf_op jit(solution)/shard_map/ppermute | solution.py:424
  33.2 3.9 %collective-permute-start.7 = (bf16[4,64,256]{2,1,0:T(8,128)(2,1)S(1)}, bf16[4,64,256]{2,1,0:T(8,128)(2,1)S(1)}, u32[]{:S(2)}, u32[]{:S(2)}) collective-permute-start(bf16[4,64,256]{2,1,0:T(8,128)(2,1)S(1)} %collective-permute-done.5.far_ref), channel_id=1, source_target_pairs={{0,1},{1,0},{2,3},{3,2},{4,5},{5,4},{6,7},{7,6},{8,9},{9,8},{10,11... | collective-permute-start | bytes 393224 | tf_op jit(solution)/shard_map/ppermute | solution.py:424
  33.2 13.2 %collective-permute-start = (bf16[32,1792]{1,0:T(8,128)(2,1)}, bf16[32,1792]{1,0:T(8,128)(2,1)S(1)}, u32[]{:S(2)}, u32[]{:S(2)}) collective-permute-start(bf16[32,1792]{1,0:T(8,128)(2,1)} %get-tuple-element.22), channel_id=1, source_target_pairs={{0,0},{1,8},{2,16},{3,24},{4,4},{5,12},{6,20},{7,28},{8,1},{9,9},{... | collective-permute-start | bytes 344072 | tf_op jit(solution)/shard_map/ppermute | solution.py:454
  34.8 11.7 %collective-permute-start.1 = (bf16[32,1792]{1,0:T(8,128)(2,1)}, bf16[32,1792]{1,0:T(8,128)(2,1)S(1)}, u32[]{:S(2)}, u32[]{:S(2)}) collective-permute-start(bf16[32,1792]{1,0:T(8,128)(2,1)} %get-tuple-element.23), channel_id=1, source_target_pairs={{0,4},{1,12},{2,20},{3,28},{4,0},{5,8},{6,16},{7,24},{8,5},{9,13},... | collective-permute-start | bytes 344072 | tf_op jit(solution)/shard_map/ppermute | solution.py:454
  46.5 20.0 %collective-permute-start.10 = (bf16[2,32,1792]{2,1,0:T(8,128)(2,1)S(1)}, bf16[2,32,1792]{2,1,0:T(8,128)(2,1)S(1)}, u32[]{:S(2)}, u32[]{:S(2)}) collective-permute-start(bf16[2,32,1792]{2,1,0:T(8,128)(2,1)S(1)} %pad_maximum_fusion.refs_0_), channel_id=1, source_target_pairs={{0,3},{1,2},{2,1},{3,0},{4,7},{5,6},{6,5},{7,4},{8,11},{9,10},{10,... | collective-permute-start | bytes 688136 | tf_op jit(solution)/shard_map/ppermute | solution.py:424
  53.2 13.3 %collective-permute-start.9 = (bf16[2,32,1792]{2,1,0:T(8,128)(2,1)S(1)}, bf16[2,32,1792]{2,1,0:T(8,128)(2,1)S(1)}, u32[]{:S(2)}, u32[]{:S(2)}) collective-permute-start(bf16[2,32,1792]{2,1,0:T(8,128)(2,1)S(1)} %pad_maximum_fusion.refs_0_), channel_id=1, source_target_pairs={{0,2},{1,3},{2,0},{3,1},{4,6},{5,7},{6,4},{7,5},{8,10},{9,11},{10,... | collective-permute-start | bytes 688136 | tf_op jit(solution)/shard_map/ppermute | solution.py:424
  56.9 9.5 %collective-permute-start.8 = (bf16[2,32,1792]{2,1,0:T(8,128)(2,1)S(1)}, bf16[2,32,1792]{2,1,0:T(8,128)(2,1)S(1)}, u32[]{:S(2)}, u32[]{:S(2)}) collective-permute-start(bf16[2,32,1792]{2,1,0:T(8,128)(2,1)S(1)} %pad_maximum_fusion.refs_0_), channel_id=1, source_target_pairs={{0,1},{1,0},{2,3},{3,2},{4,5},{5,4},{6,7},{7,6},{8,9},{9,8},{10,11... | collective-permute-start | bytes 688136 | tf_op jit(solution)/shard_map/ppermute | solution.py:424
  66.5 1.7 %copy-start = (bf16[256,4608]{1,0:T(8,128)(2,1)S(1)}, bf16[256,4608]{1,0:T(8,128)(2,1)}, u32[]{:S(2)}) copy-start(bf16[256,4608]{1,0:T(8,128)(2,1)} %all-gather.2.cloned.1.call-done.rights_ref) | copy-start | bytes 7077892
Sparse Core Ops, SparseCore 0:
  10.1 47.7 all-gather.1

commit v2 on v1

--- a/solution.py
+++ b/solution.py
@@ -8,7 +8,8 @@
 
 PANEL = 256
 CHUNK = 128
-GROUP = 64
+GROUP = 32
+SPAN = 16
 SLOTS = 3
 EXACT = lax.Precision.HIGHEST
 VMEM = pl.BlockSpec(memory_space=pltpu.VMEM)
@@ -79,36 +80,43 @@
     lane = iota((8, 128), 1)
     sub = iota((8, 128), 0)
     diagonals = []
-    for top in range(len(tiles)):
-        live = range(top, len(tiles))
-        first = base + 8 * top
+    for start in range(0, len(tiles), SPAN // 8):
         columns = [
-            {at: jnp.broadcast_to(tiles[at][:, first + q : first + q + 1], (8, 128)) for at in live}
-            for q in range(8)
+            {
+                at: jnp.broadcast_to(tiles[at][:, lane_of : lane_of + 1], (8, 128))
+                for at in range((lane_of - base) // 8, len(tiles))
+            }
+            for lane_of in range(base + 8 * start, base + 8 * start + SPAN)
         ]
-        scale = jnp.zeros((8, 128), jnp.float32)
-        pivots = jnp.zeros((8, 128), jnp.float32)
-        for q in range(8):
+        for q in range(SPAN):
+            top, own = start + q // 8, q % 8
+            first = base + 8 * start + q
+            live = range(top, len(tiles))
             column = columns[q]
-            pivot = jnp.broadcast_to(column[top][q : q + 1, :], (8, 128))
+            pivot = jnp.broadcast_to(column[top][own : own + 1, :], (8, 128))
             inverse = 1.0 / pivot
-            for k in range(q + 1, 8):
-                factor = jnp.broadcast_to(column[top][k : k + 1, :], (8, 128)) * inverse
-                for at in live:
+            for k in range(q + 1, SPAN):
+                near = start + k // 8
+                factor = jnp.broadcast_to(column[near][k % 8 : k % 8 + 1, :], (8, 128)) * inverse
+                for at in range(near, len(tiles)):
                     columns[k][at] = columns[k][at] - column[at] * factor
-            row = jnp.broadcast_to(tiles[top][q : q + 1, :], (8, 128))
-            row = jnp.where(lane == first + q, 1.0, row)
+            row = jnp.broadcast_to(tiles[top][own : own + 1, :], (8, 128))
+            row = jnp.where(lane == first, 1.0, row)
             scaled = row * inverse
             for at in live:
-                kept = jnp.where(lane == first + q, 0.0, tiles[at])
+                kept = jnp.where(lane == first, 0.0, tiles[at])
                 new = kept - column[at] * scaled
                 if at == top:
-                    new = jnp.where(sub < q, tiles[at], jnp.where(sub == q, row, new))
+                    new = jnp.where(sub < own, tiles[at], jnp.where(sub == own, row, new))
                 tiles[at] = new
-            scale = jnp.where(sub == q, lax.rsqrt(pivot), scale)
-            pivots = jnp.where(sub == q, pivot, pivots)
-        tiles[top] = tiles[top] * scale
-        diagonals.append(pivots * scale)
+            if own == 0:
+                scale = jnp.zeros((8, 128), jnp.float32)
+                pivots = jnp.zeros((8, 128), jnp.float32)
+            scale = jnp.where(sub == own, lax.rsqrt(pivot), scale)
+            pivots = jnp.where(sub == own, pivot, pivots)
+            if own == 7:
+                tiles[top] = tiles[top] * scale
+                diagonals.append(pivots * scale)
     return tiles, diagonals
 
 
@@ -470,12 +478,16 @@
             packed = jnp.concatenate([near, sums], axis=0)
     near = jnp.concatenate([near] + sums, axis=0)[None]
     order = snake(row_count, band)
-    rights = lax.all_gather(shares, "row", axis=0, tiled=True, axis_index_groups=[order])
     masks = [0]
     bit = row_count // 2
     while bit > 1:
         near = jnp.concatenate([near, exchange(near, "row", row_count, bit)], axis=0)
         masks += [held + bit for held in masks]
+        if bit == row_count // 2:
+            near, shares = lax.optimization_barrier((near, shares))
+            rights = lax.all_gather(
+                shares, "row", axis=0, tiled=True, axis_index_groups=[order]
+            )
         bit //= 2
     far = exchange(near, "row", row_count, 1)
     near_mate = exchange(near, "col", col_count, 1)
@@ -550,7 +562,7 @@
                 pltpu.SemaphoreType.DMA((count,)),
                 pltpu.SemaphoreType.DMA((SLOTS, 2)),
             ],
-            compiler_params=pltpu.CompilerParams(vmem_limit_bytes=40 * 2**20),
+            compiler_params=pltpu.CompilerParams(vmem_limit_bytes=50 * 2**20),
             cost_estimate=pl.CostEstimate(
                 flops=10**10, bytes_accessed=4 * 10**7, transcendentals=0
             ),

time: 92.5 us -> 89.7 us (0.970)
  local copies, waits for them, and re-layouts: 2.39 us -> 0.74 us
  starting transfers between devices: 23.7 us -> 25.3 us
  waiting for transfers between devices: 12.8 us -> 11.2 us
  Pallas kernels: 37.7 us -> 36.6 us
    ppermute x9, waiting for transfers between devices: 12.7 us -> 10.1 us  [exchange(): lax.ppermute(block, axis, [(place, place ^ step) for place in range(count)])]
    unnamed x2 -> x1, local copies, waits for them, and re-layouts: 1.66 us -> 0.01 us
    all_gather x1, waiting for transfers between devices: 0.02 us -> 1.06 us  [on_device(): lax.all_gather(shares, 'row', axis=0, tiled=True, axis_index_groups=[order])]
  transfers between devices with their start and end apart: 12 -> 12, of which waited for: 4 -> 6; matrix products, arithmetic and copies ran while one was open for 2% -> 1% of each run, Pallas kernels for 20% -> 19%
where the time goes in v2:
time: 89.7 us; the launch traced here: 89.4 us
  Pallas kernels  36.6 us (41%)
  starting transfers between devices  25.3 us (28%)
  between operations  14.8 us (16%)
  waiting for transfers between devices  11.2 us (12%)
    ppermute x9, starting transfers between devices, exchange(): lax.ppermute(block, axis, [(place, place ^ step) for place in range(count)])  21.2 us
    pallas_call x1, Pallas kernels, on_device(): pl.pallas_call(functools.partial(tile_kernel, (band, col_units)), out_sha...  17.6 us
    ppermute x9, waiting for transfers between devices, exchange(): lax.ppermute(block, axis, [(place, place ^ step) for place in range(count)])  10.1 us
    pallas_call x1, Pallas kernels, on_device(): pl.pallas_call(second_kernel, out_shape=(part((PANEL, PANEL)), part((dept...  8.63 us
    pallas_call x1, Pallas kernels, on_device(): pl.pallas_call(functools.partial(first_kernel, total_units, masks, band),...  8.52 us
    ppermute x2, starting transfers between devices, on_device(): moved.append(lax.ppermute(pieces[turn], ('row', 'col'), pairs))  4.03 us
    pallas_call x1, Pallas kernels, on_device(): pl.pallas_call(functools.partial(pack_kernel, band), out_shape=(jax.Shape...  1.88 us
  transfers between devices with their start and end apart: 12, of which 6 were waited for; matrix products, arithmetic and copies ran while one was open for 1% of the time, Pallas kernels for 19%

profile of v2, /device:TPU:0, one launch (start us, length us, event | category | flops | bytes accessed | tf_op | source)
XLA Modules:
  0.0 89.4 jit_solution(3619152343784054352)
XLA Ops:
  7.2 0.0 all-gather.2.cloned.1.call-start
  7.2 1.9 %shard_map.66 = (bf16[48,256]{1,0:T(8,128)(2,1)}, bf16[32,4608]{1,0:T(8,128)(2,1)}, bf16[32,1792]{1,0:T(8,128)(2,1)}, bf16[32,1792]{1,0:T(8,128)(2,1)}) custom-call(bf16[32,3584]{1,0:T(8,128)(2,1)} %keys_ref.1, bf16[32,1024]{1,0:T(8,128)(2,1)} %shifts_ref.1), custom_call_target="tpu_custom_call" | custom-call | tf_op jit(solution)/shard_map/pallas_call | solution.py:445
  9.1 2.9 %collective-permute-start.2 = (bf16[48,256]{1,0:T(8,128)(2,1)}, bf16[48,256]{1,0:T(8,128)(2,1)S(1)}, u32[]{:S(2)}, u32[]{:S(2)}) collective-permute-start(bf16[48,256]{1,0:T(8,128)(2,1)} %get-tuple-element.26), channel_id=1, source_target_pairs={{0,2},{1,3},{2,0},{3,1},{4,6},{5,7},{6,4},{7,5},{8,10},{9,11},{10,... | collective-permute-start | bytes 73736 | tf_op jit(solution)/shard_map/ppermute | solution.py:432
  12.0 0.7 slice.14
  12.8 1.3 %collective-permute-done.2 = bf16[48,256]{1,0:T(8,128)(2,1)S(1)} collective-permute-done((bf16[48,256]{1,0:T(8,128)(2,1)}, bf16[48,256]{1,0:T(8,128)(2,1)S(1)}, u32[]{:S(2)}, u32[]{:S(2)}) %collective-permute-start.2) | collective-permute-done | bytes 24608 | tf_op jit(solution)/shard_map/ppermute | solution.py:432
  14.0 0.7 slice_select_fusion
  14.8 3.1 %collective-permute-start.3 = (bf16[1,64,256]{2,1,0:T(8,128)(2,1)S(1)}, bf16[1,64,256]{2,1,0:T(8,128)(2,1)S(1)}, u32[]{:S(2)}, u32[]{:S(2)}) collective-permute-start(bf16[1,64,256]{2,1,0:T(8,128)(2,1)S(1)} %maximum_bitcast_fusion), channel_id=1, source_target_pairs={{0,16},{4,20},{8,24},{12,28},{16,0},{20,4},{24,8},{28,12},{1,17},{... | collective-permute-start | bytes 98312 | tf_op jit(solution)/shard_map/ppermute | solution.py:432
  17.9 1.9 %collective-permute-done.3 = bf16[1,64,256]{2,1,0:T(8,128)(2,1)S(1)} collective-permute-done((bf16[1,64,256]{2,1,0:T(8,128)(2,1)S(1)}, bf16[1,64,256]{2,1,0:T(8,128)(2,1)S(1)}, u32[]{:S(2)}, u32[]{:S(2)}) %collective-permute-start.3) | collective-permute-done | bytes 32800 | tf_op jit(solution)/shard_map/ppermute | solution.py:432
  19.8 0.0 all-gather.2.cloned.1.call-update
  19.8 2.0 %collective-permute-start.4 = (bf16[2,64,256]{2,1,0:T(8,128)(2,1)S(1)}, bf16[2,64,256]{2,1,0:T(8,128)(2,1)S(1)}, u32[]{:S(2)}, u32[]{:S(2)}) collective-permute-start(bf16[2,64,256]{2,1,0:T(8,128)(2,1)S(1)} %pad_maximum_fusion.1), channel_id=1, source_target_pairs={{0,8},{4,12},{8,0},{12,4},{16,24},{20,28},{24,16},{28,20},{1,9},{5... | collective-permute-start | bytes 196616 | tf_op jit(solution)/shard_map/ppermute | solution.py:432
  21.8 2.4 %collective-permute-done.4 = bf16[2,64,256]{2,1,0:T(8,128)(2,1)S(1)} collective-permute-done((bf16[2,64,256]{2,1,0:T(8,128)(2,1)S(1)}, bf16[2,64,256]{2,1,0:T(8,128)(2,1)S(1)}, u32[]{:S(2)}, u32[]{:S(2)}) %collective-permute-start.4) | collective-permute-done | bytes 65568 | tf_op jit(solution)/shard_map/ppermute | solution.py:432
  24.2 1.9 %collective-permute-start.5 = (bf16[4,64,256]{2,1,0:T(8,128)(2,1)S(1)}, bf16[4,64,256]{2,1,0:T(8,128)(2,1)S(1)}, u32[]{:S(2)}, u32[]{:S(2)}) collective-permute-start(bf16[4,64,256]{2,1,0:T(8,128)(2,1)S(1)} %constant_dynamic-update-slice_fusion.near_ref), channel_id=1, source_target_pairs={{0,4},{4,0},{8,12},{12,8},{16,20},{20,16},{24,28},{28,24},{1,5},{5... | collective-permute-start | bytes 393224 | tf_op jit(solution)/shard_map/ppermute | solution.py:432
  26.0 0.0 collective-permute-start.6
  26.0 4.4 %collective-permute-done.5.far_ref = bf16[4,64,256]{2,1,0:T(8,128)(2,1)S(1)} collective-permute-done((bf16[4,64,256]{2,1,0:T(8,128)(2,1)S(1)}, bf16[4,64,256]{2,1,0:T(8,128)(2,1)S(1)}, u32[]{:S(2)}, u32[]{:S(2)}) %collective-permute-start.5) | collective-permute-done | bytes 131104 | tf_op jit(solution)/shard_map/ppermute | solution.py:432
  30.5 0.0 collective-permute-start.7
  30.5 1.5 %collective-permute-start = (bf16[32,1792]{1,0:T(8,128)(2,1)}, bf16[32,1792]{1,0:T(8,128)(2,1)S(1)}, u32[]{:S(2)}, u32[]{:S(2)}) collective-permute-start(bf16[32,1792]{1,0:T(8,128)(2,1)} %get-tuple-element.24), channel_id=1, source_target_pairs={{0,0},{1,8},{2,16},{3,24},{4,4},{5,12},{6,20},{7,28},{8,1},{9,9},{... | collective-permute-start | bytes 344072 | tf_op jit(solution)/shard_map/ppermute | solution.py:462
  32.0 2.5 %collective-permute-start.1 = (bf16[32,1792]{1,0:T(8,128)(2,1)}, bf16[32,1792]{1,0:T(8,128)(2,1)S(1)}, u32[]{:S(2)}, u32[]{:S(2)}) collective-permute-start(bf16[32,1792]{1,0:T(8,128)(2,1)} %get-tuple-element.25), channel_id=1, source_target_pairs={{0,4},{1,12},{2,20},{3,28},{4,0},{5,8},{6,16},{7,24},{8,5},{9,13},... | collective-permute-start | bytes 344072 | tf_op jit(solution)/shard_map/ppermute | solution.py:462
  35.2 0.0 collective-permute-done.6.near_mate_ref
  35.2 0.0 collective-permute-done.7.far_mate_ref
  35.2 8.5 %shard_map.67 = (f32[8,128]{1,0:T(8,128)S(1)}, f32[256,256]{1,0:T(8,128)S(1)}, f32[256,256]{1,0:T(8,128)S(1)}, bf16[256,512]{1,0:T(8,128)(2,1)S(1)}, f32[2,128,5...) custom-call(f32[1]{0:T(128)S(6)} %copy.8.ridge_ref, ...), custom_call_target="tpu_custom_call" | custom-call | flops 10000000000 | bytes 1000000 | tf_op jit(solution)/shard_map/pallas_call | solution.py:499
  43.7 0.0 collective-permute-done
  43.7 0.0 collective-permute-done.1
  43.8 7.1 %collective-permute-start.10 = (bf16[2,32,1792]{2,1,0:T(8,128)(2,1)S(1)}, bf16[2,32,1792]{2,1,0:T(8,128)(2,1)S(1)}, u32[]{:S(2)}, u32[]{:S(2)}) collective-permute-start(bf16[2,32,1792]{2,1,0:T(8,128)(2,1)S(1)} %pad_maximum_fusion.refs_0_), channel_id=1, source_target_pairs={{0,3},{1,2},{2,1},{3,0},{4,7},{5,6},{6,5},{7,4},{8,11},{9,10},{10,... | collective-permute-start | bytes 688136 | tf_op jit(solution)/shard_map/ppermute | solution.py:432
  50.8 4.2 %collective-permute-start.9 = (bf16[2,32,1792]{2,1,0:T(8,128)(2,1)S(1)}, bf16[2,32,1792]{2,1,0:T(8,128)(2,1)S(1)}, u32[]{:S(2)}, u32[]{:S(2)}) collective-permute-start(bf16[2,32,1792]{2,1,0:T(8,128)(2,1)S(1)} %pad_maximum_fusion.refs_0_), channel_id=1, source_target_pairs={{0,2},{1,3},{2,0},{3,1},{4,6},{5,7},{6,4},{7,5},{8,10},{9,11},{10,... | collective-permute-start | bytes 688136 | tf_op jit(solution)/shard_map/ppermute | solution.py:432
  55.0 0.0 collective-permute-start.8
  55.1 8.6 %shard_map.68 = (f32[256,256]{1,0:T(8,128)S(1)}, f32[256,256]{1,0:T(8,128)S(1)}, bf16[256,512]{1,0:T(8,128)(2,1)S(1)}, bf16[3,256,256]{2,1,0:T(8,128)(2,1)S(1)}) custom-call(f32[8,128]{1,0:T(8,128)S(1)} %get-tuple-element.30.amount_ref, f32[2,128,512]{2,1,0:T(8,128)S(1)} %get-tuple-element.31.carried_ref, f32[256,256]{1,0:T(8,128)S(1)} %get-tuple-element.32.middle_ref, ...), custom_call_target="tpu_custom_call" | custom-call | flops 10000000000 | bytes 1000000 | tf_op jit(solution)/shard_map/pallas_call | solution.py:524
  63.7 0.0 collective-permute-done.10.refs_3_
  63.7 0.2 collective-permute-done.9.refs_2_
  63.9 0.0 collective-permute-done.8.refs_1_
  63.9 1.1 %all-gather.2.cloned.1.call-done.rights_ref = bf16[256,4608]{1,0:T(8,128)(2,1)} async-done(((bf16[32,4608]{1,0:T(8,128)(2,1)}), bf16[256,4608]{1,0:T(8,128)(2,1)}) %all-gather.2.cloned.1.call-update) | async-done | bytes 2359312 | tf_op jit(solution)/shard_map/all_gather | solution.py:488
  64.9 17.6 %shard_map.69 = (f32[1792,256]{1,0:T(8,128)}, f32[1792,256]{1,0:T(8,128)}, f32[1792,3584]{1,0:T(8,128)}, f32[1792,1024]{1,0:T(8,128)}) custom-call(f32[8,128]{1,0:T(8,128)S(1)} %get-tuple-element.30.amount_ref, bf16[3,256,256]{2,1,0:T(8,128)(2,1)S(1)} %get-tuple-element.34.terms_ref, bf16[256,512]{1,0:T(8,128)(2,1)S(1)} %get-tuple-element.35.heads_a_ref, ...), custom_call_target="tpu_custom_call" | custom-call | flops 10000000000 | bytes 40000000 | tf_op jit(solution)/shard_map/pallas_call | solution.py:546
  (6 shorter events, 0.1 us)
Async XLA Ops:
  7.2 57.8 %all-gather.2.cloned.1.call-start = ((), (), s32[]{:S(2)}) async-start(), calls=%async_computation | async-start | bytes 2654208 | tf_op jit(solution)/shard_map/all_gather | solution.py:488
  9.1 5.0 %collective-permute-start.2 = (bf16[48,256]{1,0:T(8,128)(2,1)}, bf16[48,256]{1,0:T(8,128)(2,1)S(1)}, u32[]{:S(2)}, u32[]{:S(2)}) collective-permute-start(bf16[48,256]{1,0:T(8,128)(2,1)} %get-tuple-element.26), channel_id=1, source_target_pairs={{0,2},{1,3},{2,0},{3,1},{4,6},{5,7},{6,4},{7,5},{8,10},{9,11},{10,... | collective-permute-start | bytes 73736 | tf_op jit(solution)/shard_map/ppermute | solution.py:432
  14.8 5.0 %collective-permute-start.3 = (bf16[1,64,256]{2,1,0:T(8,128)(2,1)S(1)}, bf16[1,64,256]{2,1,0:T(8,128)(2,1)S(1)}, u32[]{:S(2)}, u32[]{:S(2)}) collective-permute-start(bf16[1,64,256]{2,1,0:T(8,128)(2,1)S(1)} %maximum_bitcast_fusion), channel_id=1, source_target_pairs={{0,16},{4,20},{8,24},{12,28},{16,0},{20,4},{24,8},{28,12},{1,17},{... | collective-permute-start | bytes 98312 | tf_op jit(solution)/shard_map/ppermute | solution.py:432
  19.8 4.3 %collective-permute-start.4 = (bf16[2,64,256]{2,1,0:T(8,128)(2,1)S(1)}, bf16[2,64,256]{2,1,0:T(8,128)(2,1)S(1)}, u32[]{:S(2)}, u32[]{:S(2)}) collective-permute-start(bf16[2,64,256]{2,1,0:T(8,128)(2,1)S(1)} %pad_maximum_fusion.1), channel_id=1, source_target_pairs={{0,8},{4,12},{8,0},{12,4},{16,24},{20,28},{24,16},{28,20},{1,9},{5... | collective-permute-start | bytes 196616 | tf_op jit(solution)/shard_map/ppermute | solution.py:432
  24.2 6.3 %collective-permute-start.5 = (bf16[4,64,256]{2,1,0:T(8,128)(2,1)S(1)}, bf16[4,64,256]{2,1,0:T(8,128)(2,1)S(1)}, u32[]{:S(2)}, u32[]{:S(2)}) collective-permute-start(bf16[4,64,256]{2,1,0:T(8,128)(2,1)S(1)} %constant_dynamic-update-slice_fusion.near_ref), channel_id=1, source_target_pairs={{0,4},{4,0},{8,12},{12,8},{16,20},{20,16},{24,28},{28,24},{1,5},{5... | collective-permute-start | bytes 393224 | tf_op jit(solution)/shard_map/ppermute | solution.py:432
  26.0 9.1 %collective-permute-start.6 = (bf16[4,64,256]{2,1,0:T(8,128)(2,1)S(1)}, bf16[4,64,256]{2,1,0:T(8,128)(2,1)S(1)}, u32[]{:S(2)}, u32[]{:S(2)}) collective-permute-start(bf16[4,64,256]{2,1,0:T(8,128)(2,1)S(1)} %constant_dynamic-update-slice_fusion.near_ref), channel_id=1, source_target_pairs={{0,1},{1,0},{2,3},{3,2},{4,5},{5,4},{6,7},{7,6},{8,9},{9,8},{10,11... | collective-permute-start | bytes 393224 | tf_op jit(solution)/shard_map/ppermute | solution.py:432
  30.5 4.7 %collective-permute-start.7 = (bf16[4,64,256]{2,1,0:T(8,128)(2,1)S(1)}, bf16[4,64,256]{2,1,0:T(8,128)(2,1)S(1)}, u32[]{:S(2)}, u32[]{:S(2)}) collective-permute-start(bf16[4,64,256]{2,1,0:T(8,128)(2,1)S(1)} %collective-permute-done.5.far_ref), channel_id=1, source_target_pairs={{0,1},{1,0},{2,3},{3,2},{4,5},{5,4},{6,7},{7,6},{8,9},{9,8},{10,11... | collective-permute-start | bytes 393224 | tf_op jit(solution)/shard_map/ppermute | solution.py:432
  30.5 13.2 %collective-permute-start = (bf16[32,1792]{1,0:T(8,128)(2,1)}, bf16[32,1792]{1,0:T(8,128)(2,1)S(1)}, u32[]{:S(2)}, u32[]{:S(2)}) collective-permute-start(bf16[32,1792]{1,0:T(8,128)(2,1)} %get-tuple-element.24), channel_id=1, source_target_pairs={{0,0},{1,8},{2,16},{3,24},{4,4},{5,12},{6,20},{7,28},{8,1},{9,9},{... | collective-permute-start | bytes 344072 | tf_op jit(solution)/shard_map/ppermute | solution.py:462
  32.0 11.7 %collective-permute-start.1 = (bf16[32,1792]{1,0:T(8,128)(2,1)}, bf16[32,1792]{1,0:T(8,128)(2,1)S(1)}, u32[]{:S(2)}, u32[]{:S(2)}) collective-permute-start(bf16[32,1792]{1,0:T(8,128)(2,1)} %get-tuple-element.25), channel_id=1, source_target_pairs={{0,4},{1,12},{2,20},{3,28},{4,0},{5,8},{6,16},{7,24},{8,5},{9,13},... | collective-permute-start | bytes 344072 | tf_op jit(solution)/shard_map/ppermute | solution.py:462
  43.8 20.0 %collective-permute-start.10 = (bf16[2,32,1792]{2,1,0:T(8,128)(2,1)S(1)}, bf16[2,32,1792]{2,1,0:T(8,128)(2,1)S(1)}, u32[]{:S(2)}, u32[]{:S(2)}) collective-permute-start(bf16[2,32,1792]{2,1,0:T(8,128)(2,1)S(1)} %pad_maximum_fusion.refs_0_), channel_id=1, source_target_pairs={{0,3},{1,2},{2,1},{3,0},{4,7},{5,6},{6,5},{7,4},{8,11},{9,10},{10,... | collective-permute-start | bytes 688136 | tf_op jit(solution)/shard_map/ppermute | solution.py:432
  50.8 13.0 %collective-permute-start.9 = (bf16[2,32,1792]{2,1,0:T(8,128)(2,1)S(1)}, bf16[2,32,1792]{2,1,0:T(8,128)(2,1)S(1)}, u32[]{:S(2)}, u32[]{:S(2)}) collective-permute-start(bf16[2,32,1792]{2,1,0:T(8,128)(2,1)S(1)} %pad_maximum_fusion.refs_0_), channel_id=1, source_target_pairs={{0,2},{1,3},{2,0},{3,1},{4,6},{5,7},{6,4},{7,5},{8,10},{9,11},{10,... | collective-permute-start | bytes 688136 | tf_op jit(solution)/shard_map/ppermute | solution.py:432
  55.0 8.8 %collective-permute-start.8 = (bf16[2,32,1792]{2,1,0:T(8,128)(2,1)S(1)}, bf16[2,32,1792]{2,1,0:T(8,128)(2,1)S(1)}, u32[]{:S(2)}, u32[]{:S(2)}) collective-permute-start(bf16[2,32,1792]{2,1,0:T(8,128)(2,1)S(1)} %pad_maximum_fusion.refs_0_), channel_id=1, source_target_pairs={{0,1},{1,0},{2,3},{3,2},{4,5},{5,4},{6,7},{7,6},{8,9},{9,8},{10,11... | collective-permute-start | bytes 688136 | tf_op jit(solution)/shard_map/ppermute | solution.py:432
Sparse Core Ops, SparseCore 0:
  19.9 44.9 all-gather.1

commit v3 on v2

--- a/solution.py
+++ b/solution.py
@@ -51,9 +51,8 @@
     return wide[0:8, 0:128] + wide[0:8, 128:256] + wide[8:16, 0:128]
 
 
-def pack_kernel(band, keys_ref, shifts_ref, packed_ref, rights_ref, *piece_refs):
+def pack_kernel(keys_ref, packed_ref):
     rows, units = keys_ref.shape
-    row_units = units // band
     packed_ref[0:rows, :] = keys_ref[:, 0:PANEL]
     sums = jnp.zeros((8, 128), jnp.float32)
     for lane in range(0, units, 128):
@@ -62,6 +61,11 @@
         for top in range(0, rows, 8):
             sums = sums + squares[top : top + 8]
     store_sums(packed_ref, rows, sums)
+
+
+def shares_kernel(band, keys_ref, shifts_ref, rights_ref, *piece_refs):
+    units = keys_ref.shape[1]
+    row_units = units // band
     rights_ref[:, 0:units] = keys_ref[...]
     rights_ref[:, units:] = shifts_ref[...]
     for turn in range(band):
@@ -326,6 +330,12 @@
         high = value.astype(jnp.bfloat16)
         right[step % 2, 0:depth, :] = high
         right[step % 2, depth:, :] = (value - high.astype(jnp.float32)).astype(jnp.bfloat16)
+        if step == 0:
+
+            @pl.when(col_index < 2)
+            def _():
+                right[0, :, 0:PANEL] = jnp.zeros((2 * depth, PANEL), jnp.bfloat16)
+
 
     def copies(step):
         slot = step % SLOTS
@@ -364,12 +374,6 @@
         @pl.when(in_a | in_b)
         def _():
             out[slot, 0:PANEL, :] = jnp.zeros((PANEL, width), jnp.float32)
-
-        if step == 0:
-
-            @pl.when(col_index < 2)
-            def _():
-                out[slot, :, 0:PANEL] = jnp.zeros((row_units, PANEL), jnp.float32)
 
     def finish_forward(step, slot):
         for here, heads in ((in_a, heads_a_ref), (in_b, heads_b_ref)):
@@ -442,15 +446,18 @@
     row_units = total_units // row_count
     band = row_count // col_count
 
-    packed, shares, *pieces = pl.pallas_call(
-        functools.partial(pack_kernel, band),
-        out_shape=(
-            jax.ShapeDtypeStruct((rows + 16, PANEL), jnp.bfloat16),
-            jax.ShapeDtypeStruct((rows, col_units + shift_cols), jnp.bfloat16),
-        )
+    packed = pl.pallas_call(
+        pack_kernel,
+        out_shape=jax.ShapeDtypeStruct((rows + 16, PANEL), jnp.bfloat16),
+        in_specs=[VMEM],
+        out_specs=VMEM,
+    )(edit_keys)
+    shares, *pieces = pl.pallas_call(
+        functools.partial(shares_kernel, band),
+        out_shape=(jax.ShapeDtypeStruct((rows, col_units + shift_cols), jnp.bfloat16),)
         + (jax.ShapeDtypeStruct((rows, row_units), jnp.bfloat16),) * band,
         in_specs=[VMEM, VMEM],
-        out_specs=(VMEM,) * (2 + band),
+        out_specs=(VMEM,) * (1 + band),
     )(edit_keys, edit_shifts)
     moved = []
     for turn in range(band):

time: 89.7 us -> 89.4 us (level)
  waiting for transfers between devices: 11.2 us -> 9.47 us
  Pallas kernels: 36.6 us -> 38.1 us
    ppermute x9, waiting for transfers between devices: 10.1 us -> 8.36 us  [exchange(): lax.ppermute(block, axis, [(place, place ^ step) for place in range(count)])]
    pallas_call x1 -> x2, Pallas kernels: 1.88 us -> 3.45 us  [the longest x1 1.77 us: on_device(): pl.pallas_call(functools.partial(shares_kernel, band), out_shape=(jax.Sha...]
  transfers between devices with their start and end apart: 12 -> 12, of which waited for: 6 -> 6; matrix products, arithmetic and copies ran while one was open for 1% -> 1% of each run, Pallas kernels for 19% -> 21%
where the time goes in v3:
time: 89.4 us; the launch traced here: 89.1 us
  Pallas kernels  38.1 us (43%)
  starting transfers between devices  25.3 us (28%)
  between operations  14.8 us (17%)
  waiting for transfers between devices  9.47 us (11%)
    ppermute x9, starting transfers between devices, exchange(): lax.ppermute(block, axis, [(place, place ^ step) for place in range(count)])  21.2 us
    pallas_call x1, Pallas kernels, on_device(): pl.pallas_call(functools.partial(tile_kernel, (band, col_units)), out_sha...  17.5 us
    pallas_call x1, Pallas kernels, on_device(): pl.pallas_call(second_kernel, out_shape=(part((PANEL, PANEL)), part((dept...  8.63 us
    pallas_call x1, Pallas kernels, on_device(): pl.pallas_call(functools.partial(first_kernel, total_units, masks, band),...  8.51 us
    ppermute x9, waiting for transfers between devices, exchange(): lax.ppermute(block, axis, [(place, place ^ step) for place in range(count)])  8.36 us
    ppermute x2, starting transfers between devices, on_device(): moved.append(lax.ppermute(pieces[turn], ('row', 'col'), pairs))  4.03 us
  transfers between devices with their start and end apart: 12, of which 6 were waited for; matrix products, arithmetic and copies ran while one was open for 1% of the time, Pallas kernels for 21%

profile of v3, /device:TPU:0, one launch (start us, length us, event | category | flops | bytes accessed | tf_op | source)
XLA Modules:
  0.0 89.1 jit_solution(6949687617511883448)
XLA Ops:
  7.2 0.0 all-gather.2.cloned.1.call-start
  7.2 1.7 %shard_map.67 = bf16[48,256]{1,0:T(8,128)(2,1)} custom-call(bf16[32,3584]{1,0:T(8,128)(2,1)} %keys_ref.3), custom_call_target="tpu_custom_call" | custom-call | tf_op jit(solution)/shard_map/pallas_call | solution.py:449
  8.9 2.9 %collective-permute-start.2 = (bf16[48,256]{1,0:T(8,128)(2,1)}, bf16[48,256]{1,0:T(8,128)(2,1)S(1)}, u32[]{:S(2)}, u32[]{:S(2)}) collective-permute-start(bf16[48,256]{1,0:T(8,128)(2,1)} %shard_map.67), channel_id=1, source_target_pairs={{0,2},{1,3},{2,0},{3,1},{4,6},{5,7},{6,4},{7,5},{8,10},{9,11},{10,... | collective-permute-start | bytes 73736 | tf_op jit(solution)/shard_map/ppermute | solution.py:436
  11.8 0.7 slice.18
  12.6 1.3 %collective-permute-done.2 = bf16[48,256]{1,0:T(8,128)(2,1)S(1)} collective-permute-done((bf16[48,256]{1,0:T(8,128)(2,1)}, bf16[48,256]{1,0:T(8,128)(2,1)S(1)}, u32[]{:S(2)}, u32[]{:S(2)}) %collective-permute-start.2) | collective-permute-done | bytes 24608 | tf_op jit(solution)/shard_map/ppermute | solution.py:436
  13.8 0.7 slice_select_fusion
  14.6 3.1 %collective-permute-start.3 = (bf16[1,64,256]{2,1,0:T(8,128)(2,1)S(1)}, bf16[1,64,256]{2,1,0:T(8,128)(2,1)S(1)}, u32[]{:S(2)}, u32[]{:S(2)}) collective-permute-start(bf16[1,64,256]{2,1,0:T(8,128)(2,1)S(1)} %maximum_bitcast_fusion), channel_id=1, source_target_pairs={{0,16},{4,20},{8,24},{12,28},{16,0},{20,4},{24,8},{28,12},{1,17},{... | collective-permute-start | bytes 98312 | tf_op jit(solution)/shard_map/ppermute | solution.py:436
  17.7 1.8 %shard_map.66 = (bf16[32,4608]{1,0:T(8,128)(2,1)}, bf16[32,1792]{1,0:T(8,128)(2,1)}, bf16[32,1792]{1,0:T(8,128)(2,1)}) custom-call(bf16[32,3584]{1,0:T(8,128)(2,1)} %keys_ref.3, bf16[32,1024]{1,0:T(8,128)(2,1)} %shifts_ref.1), custom_call_target="tpu_custom_call" | custom-call | tf_op jit(solution)/shard_map/pallas_call | solution.py:455
  19.5 0.1 collective-permute-done.3
  19.6 0.0 all-gather.2.cloned.1.call-update
  19.6 2.0 %collective-permute-start.4 = (bf16[2,64,256]{2,1,0:T(8,128)(2,1)S(1)}, bf16[2,64,256]{2,1,0:T(8,128)(2,1)S(1)}, u32[]{:S(2)}, u32[]{:S(2)}) collective-permute-start(bf16[2,64,256]{2,1,0:T(8,128)(2,1)S(1)} %pad_maximum_fusion.1), channel_id=1, source_target_pairs={{0,8},{4,12},{8,0},{12,4},{16,24},{20,28},{24,16},{28,20},{1,9},{5... | collective-permute-start | bytes 196616 | tf_op jit(solution)/shard_map/ppermute | solution.py:436
  21.6 2.4 %collective-permute-done.4 = bf16[2,64,256]{2,1,0:T(8,128)(2,1)S(1)} collective-permute-done((bf16[2,64,256]{2,1,0:T(8,128)(2,1)S(1)}, bf16[2,64,256]{2,1,0:T(8,128)(2,1)S(1)}, u32[]{:S(2)}, u32[]{:S(2)}) %collective-permute-start.4) | collective-permute-done | bytes 65568 | tf_op jit(solution)/shard_map/ppermute | solution.py:436
  24.0 1.9 %collective-permute-start.5 = (bf16[4,64,256]{2,1,0:T(8,128)(2,1)S(1)}, bf16[4,64,256]{2,1,0:T(8,128)(2,1)S(1)}, u32[]{:S(2)}, u32[]{:S(2)}) collective-permute-start(bf16[4,64,256]{2,1,0:T(8,128)(2,1)S(1)} %constant_dynamic-update-slice_fusion.near_ref), channel_id=1, source_target_pairs={{0,4},{4,0},{8,12},{12,8},{16,20},{20,16},{24,28},{28,24},{1,5},{5... | collective-permute-start | bytes 393224 | tf_op jit(solution)/shard_map/ppermute | solution.py:436
  25.8 0.0 collective-permute-start.6
  25.8 4.4 %collective-permute-done.5.far_ref = bf16[4,64,256]{2,1,0:T(8,128)(2,1)S(1)} collective-permute-done((bf16[4,64,256]{2,1,0:T(8,128)(2,1)S(1)}, bf16[4,64,256]{2,1,0:T(8,128)(2,1)S(1)}, u32[]{:S(2)}, u32[]{:S(2)}) %collective-permute-start.5) | collective-permute-done | bytes 131104 | tf_op jit(solution)/shard_map/ppermute | solution.py:436
  30.3 0.0 collective-permute-start.7
  30.3 1.5 %collective-permute-start = (bf16[32,1792]{1,0:T(8,128)(2,1)}, bf16[32,1792]{1,0:T(8,128)(2,1)S(1)}, u32[]{:S(2)}, u32[]{:S(2)}) collective-permute-start(bf16[32,1792]{1,0:T(8,128)(2,1)} %get-tuple-element.23), channel_id=1, source_target_pairs={{0,0},{1,8},{2,16},{3,24},{4,4},{5,12},{6,20},{7,28},{8,1},{9,9},{... | collective-permute-start | bytes 344072 | tf_op jit(solution)/shard_map/ppermute | solution.py:469
  31.8 2.5 %collective-permute-start.1 = (bf16[32,1792]{1,0:T(8,128)(2,1)}, bf16[32,1792]{1,0:T(8,128)(2,1)S(1)}, u32[]{:S(2)}, u32[]{:S(2)}) collective-permute-start(bf16[32,1792]{1,0:T(8,128)(2,1)} %get-tuple-element.24), channel_id=1, source_target_pairs={{0,4},{1,12},{2,20},{3,28},{4,0},{5,8},{6,16},{7,24},{8,5},{9,13},... | collective-permute-start | bytes 344072 | tf_op jit(solution)/shard_map/ppermute | solution.py:469
  34.9 0.0 collective-permute-done.6.near_mate_ref
  35.0 0.0 collective-permute-done.7.far_mate_ref
  35.0 8.5 %shard_map.68 = (f32[8,128]{1,0:T(8,128)S(1)}, f32[256,256]{1,0:T(8,128)S(1)}, f32[256,256]{1,0:T(8,128)S(1)}, bf16[256,512]{1,0:T(8,128)(2,1)S(1)}, f32[2,128,5...) custom-call(f32[1]{0:T(128)S(6)} %copy.8.ridge_ref, ...), custom_call_target="tpu_custom_call" | custom-call | flops 10000000000 | bytes 1000000 | tf_op jit(solution)/shard_map/pallas_call | solution.py:506
  43.5 0.0 collective-permute-done
  43.5 0.0 collective-permute-done.1
  43.5 7.1 %collective-permute-start.10 = (bf16[2,32,1792]{2,1,0:T(8,128)(2,1)S(1)}, bf16[2,32,1792]{2,1,0:T(8,128)(2,1)S(1)}, u32[]{:S(2)}, u32[]{:S(2)}) collective-permute-start(bf16[2,32,1792]{2,1,0:T(8,128)(2,1)S(1)} %pad_maximum_fusion.refs_0_), channel_id=1, source_target_pairs={{0,3},{1,2},{2,1},{3,0},{4,7},{5,6},{6,5},{7,4},{8,11},{9,10},{10,... | collective-permute-start | bytes 688136 | tf_op jit(solution)/shard_map/ppermute | solution.py:436
  50.6 4.2 %collective-permute-start.9 = (bf16[2,32,1792]{2,1,0:T(8,128)(2,1)S(1)}, bf16[2,32,1792]{2,1,0:T(8,128)(2,1)S(1)}, u32[]{:S(2)}, u32[]{:S(2)}) collective-permute-start(bf16[2,32,1792]{2,1,0:T(8,128)(2,1)S(1)} %pad_maximum_fusion.refs_0_), channel_id=1, source_target_pairs={{0,2},{1,3},{2,0},{3,1},{4,6},{5,7},{6,4},{7,5},{8,10},{9,11},{10,... | collective-permute-start | bytes 688136 | tf_op jit(solution)/shard_map/ppermute | solution.py:436
  54.8 0.0 collective-permute-start.8
  54.9 8.6 %shard_map.69 = (f32[256,256]{1,0:T(8,128)S(1)}, f32[256,256]{1,0:T(8,128)S(1)}, bf16[256,512]{1,0:T(8,128)(2,1)S(1)}, bf16[3,256,256]{2,1,0:T(8,128)(2,1)S(1)}) custom-call(f32[8,128]{1,0:T(8,128)S(1)} %get-tuple-element.28.amount_ref, f32[2,128,512]{2,1,0:T(8,128)S(1)} %get-tuple-element.29.carried_ref, f32[256,256]{1,0:T(8,128)S(1)} %get-tuple-element.30.middle_ref, ...), custom_call_target="tpu_custom_call" | custom-call | flops 10000000000 | bytes 1000000 | tf_op jit(solution)/shard_map/pallas_call | solution.py:531
  63.5 0.0 collective-permute-done.10.refs_3_
  63.5 0.2 collective-permute-done.9.refs_2_
  63.7 0.0 collective-permute-done.8.refs_1_
  63.7 1.1 %all-gather.2.cloned.1.call-done.rights_ref = bf16[256,4608]{1,0:T(8,128)(2,1)} async-done(((bf16[32,4608]{1,0:T(8,128)(2,1)}), bf16[256,4608]{1,0:T(8,128)(2,1)}) %all-gather.2.cloned.1.call-update) | async-done | bytes 2359312 | tf_op jit(solution)/shard_map/all_gather | solution.py:495
  64.7 17.5 %shard_map.70 = (f32[1792,256]{1,0:T(8,128)}, f32[1792,256]{1,0:T(8,128)}, f32[1792,3584]{1,0:T(8,128)}, f32[1792,1024]{1,0:T(8,128)}) custom-call(f32[8,128]{1,0:T(8,128)S(1)} %get-tuple-element.28.amount_ref, bf16[3,256,256]{2,1,0:T(8,128)(2,1)S(1)} %get-tuple-element.32.terms_ref, bf16[256,512]{1,0:T(8,128)(2,1)S(1)} %get-tuple-element.33.heads_a_ref, ...), custom_call_target="tpu_custom_call" | custom-call | flops 10000000000 | bytes 40000000 | tf_op jit(solution)/shard_map/pallas_call | solution.py:553
  (6 shorter events, 0.1 us)
Async XLA Ops:
  7.2 57.6 %all-gather.2.cloned.1.call-start = ((), (), s32[]{:S(2)}) async-start(), calls=%async_computation | async-start | bytes 2654208 | tf_op jit(solution)/shard_map/all_gather | solution.py:495
  8.9 5.0 %collective-permute-start.2 = (bf16[48,256]{1,0:T(8,128)(2,1)}, bf16[48,256]{1,0:T(8,128)(2,1)S(1)}, u32[]{:S(2)}, u32[]{:S(2)}) collective-permute-start(bf16[48,256]{1,0:T(8,128)(2,1)} %shard_map.67), channel_id=1, source_target_pairs={{0,2},{1,3},{2,0},{3,1},{4,6},{5,7},{6,4},{7,5},{8,10},{9,11},{10,... | collective-permute-start | bytes 73736 | tf_op jit(solution)/shard_map/ppermute | solution.py:436
  14.6 5.0 %collective-permute-start.3 = (bf16[1,64,256]{2,1,0:T(8,128)(2,1)S(1)}, bf16[1,64,256]{2,1,0:T(8,128)(2,1)S(1)}, u32[]{:S(2)}, u32[]{:S(2)}) collective-permute-start(bf16[1,64,256]{2,1,0:T(8,128)(2,1)S(1)} %maximum_bitcast_fusion), channel_id=1, source_target_pairs={{0,16},{4,20},{8,24},{12,28},{16,0},{20,4},{24,8},{28,12},{1,17},{... | collective-permute-start | bytes 98312 | tf_op jit(solution)/shard_map/ppermute | solution.py:436
  19.6 4.3 %collective-permute-start.4 = (bf16[2,64,256]{2,1,0:T(8,128)(2,1)S(1)}, bf16[2,64,256]{2,1,0:T(8,128)(2,1)S(1)}, u32[]{:S(2)}, u32[]{:S(2)}) collective-permute-start(bf16[2,64,256]{2,1,0:T(8,128)(2,1)S(1)} %pad_maximum_fusion.1), channel_id=1, source_target_pairs={{0,8},{4,12},{8,0},{12,4},{16,24},{20,28},{24,16},{28,20},{1,9},{5... | collective-permute-start | bytes 196616 | tf_op jit(solution)/shard_map/ppermute | solution.py:436
  24.0 6.3 %collective-permute-start.5 = (bf16[4,64,256]{2,1,0:T(8,128)(2,1)S(1)}, bf16[4,64,256]{2,1,0:T(8,128)(2,1)S(1)}, u32[]{:S(2)}, u32[]{:S(2)}) collective-permute-start(bf16[4,64,256]{2,1,0:T(8,128)(2,1)S(1)} %constant_dynamic-update-slice_fusion.near_ref), channel_id=1, source_target_pairs={{0,4},{4,0},{8,12},{12,8},{16,20},{20,16},{24,28},{28,24},{1,5},{5... | collective-permute-start | bytes 393224 | tf_op jit(solution)/shard_map/ppermute | solution.py:436
  25.8 9.1 %collective-permute-start.6 = (bf16[4,64,256]{2,1,0:T(8,128)(2,1)S(1)}, bf16[4,64,256]{2,1,0:T(8,128)(2,1)S(1)}, u32[]{:S(2)}, u32[]{:S(2)}) collective-permute-start(bf16[4,64,256]{2,1,0:T(8,128)(2,1)S(1)} %constant_dynamic-update-slice_fusion.near_ref), channel_id=1, source_target_pairs={{0,1},{1,0},{2,3},{3,2},{4,5},{5,4},{6,7},{7,6},{8,9},{9,8},{10,11... | collective-permute-start | bytes 393224 | tf_op jit(solution)/shard_map/ppermute | solution.py:436
  30.3 4.7 %collective-permute-start.7 = (bf16[4,64,256]{2,1,0:T(8,128)(2,1)S(1)}, bf16[4,64,256]{2,1,0:T(8,128)(2,1)S(1)}, u32[]{:S(2)}, u32[]{:S(2)}) collective-permute-start(bf16[4,64,256]{2,1,0:T(8,128)(2,1)S(1)} %collective-permute-done.5.far_ref), channel_id=1, source_target_pairs={{0,1},{1,0},{2,3},{3,2},{4,5},{5,4},{6,7},{7,6},{8,9},{9,8},{10,11... | collective-permute-start | bytes 393224 | tf_op jit(solution)/shard_map/ppermute | solution.py:436
  30.3 13.2 %collective-permute-start = (bf16[32,1792]{1,0:T(8,128)(2,1)}, bf16[32,1792]{1,0:T(8,128)(2,1)S(1)}, u32[]{:S(2)}, u32[]{:S(2)}) collective-permute-start(bf16[32,1792]{1,0:T(8,128)(2,1)} %get-tuple-element.23), channel_id=1, source_target_pairs={{0,0},{1,8},{2,16},{3,24},{4,4},{5,12},{6,20},{7,28},{8,1},{9,9},{... | collective-permute-start | bytes 344072 | tf_op jit(solution)/shard_map/ppermute | solution.py:469
  31.8 11.7 %collective-permute-start.1 = (bf16[32,1792]{1,0:T(8,128)(2,1)}, bf16[32,1792]{1,0:T(8,128)(2,1)S(1)}, u32[]{:S(2)}, u32[]{:S(2)}) collective-permute-start(bf16[32,1792]{1,0:T(8,128)(2,1)} %get-tuple-element.24), channel_id=1, source_target_pairs={{0,4},{1,12},{2,20},{3,28},{4,0},{5,8},{6,16},{7,24},{8,5},{9,13},... | collective-permute-start | bytes 344072 | tf_op jit(solution)/shard_map/ppermute | solution.py:469
  43.5 20.0 %collective-permute-start.10 = (bf16[2,32,1792]{2,1,0:T(8,128)(2,1)S(1)}, bf16[2,32,1792]{2,1,0:T(8,128)(2,1)S(1)}, u32[]{:S(2)}, u32[]{:S(2)}) collective-permute-start(bf16[2,32,1792]{2,1,0:T(8,128)(2,1)S(1)} %pad_maximum_fusion.refs_0_), channel_id=1, source_target_pairs={{0,3},{1,2},{2,1},{3,0},{4,7},{5,6},{6,5},{7,4},{8,11},{9,10},{10,... | collective-permute-start | bytes 688136 | tf_op jit(solution)/shard_map/ppermute | solution.py:436
  50.6 13.0 %collective-permute-start.9 = (bf16[2,32,1792]{2,1,0:T(8,128)(2,1)S(1)}, bf16[2,32,1792]{2,1,0:T(8,128)(2,1)S(1)}, u32[]{:S(2)}, u32[]{:S(2)}) collective-permute-start(bf16[2,32,1792]{2,1,0:T(8,128)(2,1)S(1)} %pad_maximum_fusion.refs_0_), channel_id=1, source_target_pairs={{0,2},{1,3},{2,0},{3,1},{4,6},{5,7},{6,4},{7,5},{8,10},{9,11},{10,... | collective-permute-start | bytes 688136 | tf_op jit(solution)/shard_map/ppermute | solution.py:436
  54.8 8.8 %collective-permute-start.8 = (bf16[2,32,1792]{2,1,0:T(8,128)(2,1)S(1)}, bf16[2,32,1792]{2,1,0:T(8,128)(2,1)S(1)}, u32[]{:S(2)}, u32[]{:S(2)}) collective-permute-start(bf16[2,32,1792]{2,1,0:T(8,128)(2,1)S(1)} %pad_maximum_fusion.refs_0_), channel_id=1, source_target_pairs={{0,1},{1,0},{2,3},{3,2},{4,5},{5,4},{6,7},{7,6},{8,9},{9,8},{10,11... | collective-permute-start | bytes 688136 | tf_op jit(solution)/shard_map/ppermute | solution.py:436
Sparse Core Ops, SparseCore 0:
  19.7 44.9 all-gather.1
